TPU v7x, 32 devices: a whole 2x2x4 slice. The times are simulated.
32 devices in a mesh: seg: 8 (over y, x, core), sec: 4 (over z).
Axes of the slice: x: 2, y: 2, z: 4, core: 2. Of those that a mesh axis runs over, the one named last changes fastest.
Arguments:
- blocks: bfloat16 [8, 4, 4, 128, 128], P('seg', None, 'sec'), may hold values from -0.5 to 0.5
- left_edge: bfloat16 [4, 128], P('sec'), may hold values from -0.5 to 0.5
- right_edge: bfloat16 [4, 128], P('sec'), may hold values from -6 to 6
- occupation: int32 [1024, 8], P(None, 'seg'), may hold values from 0 to 3
- start_sector: int32 [1024], replicated, may hold values from 0 to 3
Outputs:
- amplitude: float32 [1024], replicated
All inputs are finite; a program needn't handle non-finite values.
Results may differ from a plain program's by a relative error of at most 0.015.
Values may be sent and summed in bfloat16 or wider, within the bound.
A program may use at most 64 MiB of HBM per device.

v0:
```python
import jax
import jax.numpy as jnp
from jax import lax
from jax.sharding import PartitionSpec as P


def padded_2(block, sides, width, periodic):
    for axis, dim in sides:
        count = lax.axis_size(axis)
        forward = [(i, i + 1) for i in range(count - 1)]
        if periodic:
            forward.append((count - 1, 0))
        backward = [(target, source) for source, target in forward]
        low = lax.ppermute(
            lax.slice_in_dim(block, block.shape[dim] - width, None, axis=dim), axis, forward
        )
        high = lax.ppermute(lax.slice_in_dim(block, 0, width, axis=dim), axis, backward)
        block = jnp.concatenate([low, block, high], axis=dim)
    return block


def state_masks(occ_site):
    levels = jnp.arange(4, dtype=jnp.int32)
    return (occ_site[:, None] == levels[None, :]).astype(jnp.float32)


def forward_send(vector, block_site, occ_masks):
    products = jnp.einsum("ka,nab->knb", vector, block_site, preferred_element_type=jnp.float32)
    terms = products * occ_masks[:, :, None]
    kept_term = (terms[:, 0] + terms[:, 3]).astype(jnp.bfloat16)
    upward = terms[:, 1].astype(jnp.bfloat16)
    downward = terms[:, 2].astype(jnp.bfloat16)
    return (kept_term, jnp.stack([downward, upward]))


def backward_send(vector, block_site, occ_masks):
    return (vector, jnp.stack([vector, vector]))


def forward_take(kept_term, padded, block_site, occ_masks):
    total = (
        kept_term.astype(jnp.float32)
        + padded[0].astype(jnp.float32)
        + padded[3].astype(jnp.float32)
    )
    return total.astype(jnp.bfloat16)


def backward_take(kept_term, padded, block_site, occ_masks):
    stacked = jnp.stack([kept_term, padded[3], padded[0], kept_term], axis=1)
    products = jnp.einsum("nab,knb->kna", block_site, stacked, preferred_element_type=jnp.float32)
    return jnp.sum(products * occ_masks[:, :, None], axis=1).astype(jnp.bfloat16)


def per_device(blocks, left_edge, right_edge, occupation, start_sector):
    seg_count = lax.axis_size("seg")
    half_count = seg_count // 2
    seg_index = lax.axis_index("seg")
    sec_index = lax.axis_index("sec")
    is_left = seg_index < half_count
    chain_depth = jnp.where(is_left, seg_index, seg_count - 1 - seg_index)
    is_first = chain_depth == 0
    meet_lower = seg_index == half_count - 1
    meet_upper = seg_index == half_count
    conf_count = occupation.shape[0]
    sites_here = occupation.shape[1]
    sector_width = blocks.shape[-1]
    block_count = 1
    columns = jnp.arange(sector_width, dtype=jnp.int32)
    lower_cols = (columns < sector_width // 2).astype(jnp.float32)
    upper_cols = 1.0 - lower_cols
    local_blocks = blocks[:, :, 0]
    left_row = left_edge[0]
    right_row = right_edge[0]
    batch_rows = conf_count // block_count

    def initial():
        zero_row = jnp.zeros_like(left_row)
        initial_left = jnp.where(
            (start_sector == sec_index)[:, None], left_row[None, :], zero_row[None, :]
        )
        initial_right = jnp.broadcast_to(right_row[None, :], (batch_rows, sector_width))
        return jnp.where(is_left, initial_left, initial_right)

    def run_sites(vector):
        position = jnp.where(is_left, 0, sites_here - 1)
        block_site = lax.dynamic_index_in_dim(local_blocks, position, 0, keepdims=False)
        occ_site = lax.dynamic_index_in_dim(occupation, position, 1, keepdims=False)
        occ_masks = state_masks(occ_site)
        kept_term, outgoing = lax.cond(
            is_left, forward_send, backward_send, vector, block_site, occ_masks
        )
        padded = padded_2(outgoing, (("sec", 0),), 1, True)
        vector = lax.cond(
            is_left, forward_take, backward_take, kept_term, padded, block_site, occ_masks
        )
        return vector

    section_count = half_count + block_count - 1

    def section(section_index, state_pair):
        incoming, partial_value = state_pair
        batch_index = section_index - chain_depth
        is_valid = (batch_index >= 0) & (batch_index < block_count)
        vector = jnp.where(is_first, initial(), incoming)
        vector = run_sites(vector)
        padded = padded_2(vector[None], (("seg", 0),), 1, False)
        received = jnp.where(is_left, padded[0], padded[2])
        own_vals = vector.astype(jnp.float32)
        lower_part = jnp.sum(own_vals * padded[2].astype(jnp.float32) * lower_cols[None, :], axis=1)
        upper_part = jnp.sum(own_vals * padded[0].astype(jnp.float32) * upper_cols[None, :], axis=1)
        product = jnp.where(meet_lower, lower_part, upper_part)
        previous = partial_value
        store_here = (meet_lower | meet_upper) & is_valid
        partial_value = jnp.where(store_here, product, previous)
        return (received, partial_value)

    start_state = (
        jnp.zeros((batch_rows, sector_width), jnp.bfloat16),
        jnp.zeros((conf_count,), jnp.float32),
    )
    final_state = lax.fori_loop(0, section_count, section, start_state)
    return lax.psum(final_state[1], ("seg", "sec"))


def solution(mesh):
    in_specs = (
        P("seg", None, "sec", None, None),
        P("sec", None),
        P("sec", None),
        P(None, "seg"),
        P(),
    )
    out_specs = P()
    return jax.shard_map(
        per_device, mesh=mesh, in_specs=in_specs, out_specs=out_specs, check_vma=False
    )
```

profile of v0, /device:TPU:0, one launch (start us, length us, event | category | flops | bytes accessed | tf_op | source)
XLA Modules:
  0.0 160.8 jit_solution(5362805426810196777)
XLA Ops:
  0.0 117.2 %while.18 = (s32[]{:T(128)}, bf16[1024,128]{1,0:T(8,128)(2,1)S(1)}, f32[1024]{0:T(1024)S(1)}, pred[]{:T(512)}, pred[]{:T(512)}, /*index=5*/s32[]{:T(128)}, s32[1...) while((s32[]{:T(128)}, bf16[1024,128]{1,0:T(8,128)(2,1)S(1)}, ...), condition=%wide.region_8.9_spmd.clone, body=%wide.region_0.8_spmd.clone.sunk | while | flops 274213504 | bytes 16602105 | solution.py:122
  2.3 1.8 %conditional.6 = (bf16[1024,128]{1,0:T(8,128)(2,1)S(1)}, bf16[2,1024,128]{2,1,0:T(8,128)(2,1)S(1)}) conditional(s32[]{:T(128)} %convert_element_type.171, bf16[1024,128]{1,0:T(8,128)(2,1)S(1)} %select_select_fusion.4, (bf16[1024,128]{1,0:T(8,128)(2,1)S(1)}, bf16[4,128,128]{2,1,0:T(8,128)(2,1)}, f32[1024,4]{0,1:T(4,128)S(1)}) %tuple.102), branch_computations={%region_1.1_spmd, %region_2.2_spmd} | conditional | flops 135790592 | bytes 6963216 | solution.py:90
  2.3 1.6 %fusion.24 = (bf16[1024,4,128]{2,0,1:T(8,128)(2,1)S(1)}, f32[1024,4,128]{2,0,1:T(8,128)S(1)}) fusion(f32[1024,4]{0,1:T(4,128)S(1)} %get-tuple-element.394, bf16[4,128,128]{2,1,0:T(8,128)(2,1)} %get-tuple-element.393, bf16[1024,128]{1,0:T(8,128)(2,1)S(1)} %get-tuple-element.392), kind=kOutput, calls=%fused_computation.39 | convolution fusion | flops 135266304 | bytes 3555328 | tf_op jit(solution)/shard_map/while/body/eval_jaxpr/cond/branch_1_fun/ka,nab->knb/dot_general | solution.py:28
  4.2 5.1 %collective-permute-start = (bf16[1,1024,128]{2,1,0:T(8,128)(2,1)S(1)}, bf16[1,1024,128]{2,1,0:T(8,128)(2,1)S(1)}, u32[]{:S(2)}, u32[]{:S(2)}) collective-permute-start(bf16[1,1024,128]{2,1,0:T(8,128)(2,1)S(1)} %get-tuple-element.627), channel_id=1, source_target_pairs={{1,0},{2,1},{3,2},{0,3},{5,4},{6,5},{7,6},{4,7},{9,8},{10,9},{11,1... | collective-permute-start | bytes 786440 | tf_op jit(solution)/shard_map/while/body/eval_jaxpr/ppermute | solution.py:17
  9.3 6.7 %collective-permute-done = bf16[1,1024,128]{2,1,0:T(8,128)(2,1)S(1)} collective-permute-done((bf16[1,1024,128]{2,1,0:T(8,128)(2,1)S(1)}, bf16[1,1024,128]{2,1,0:T(8,128)(2,1)S(1)}, u32[]{:S(2)}, u32[]{:S(2)}) %collective-permute-start) | collective-permute-done | bytes 262176 | tf_op jit(solution)/shard_map/while/body/eval_jaxpr/ppermute | solution.py:17
  16.0 5.4 %collective-permute-done.1 = bf16[1,1024,128]{2,1,0:T(8,128)(2,1)S(1)} collective-permute-done((bf16[1,1024,128]{2,1,0:T(8,128)(2,1)S(1)}, bf16[1,1024,128]{2,1,0:T(8,128)(2,1)S(1)}, u32[]{:S(2)}, u32[]{:S(2)}) %collective-permute-start.1) | collective-permute-done | bytes 262176 | tf_op jit(solution)/shard_map/while/body/eval_jaxpr/ppermute | solution.py:14
  21.5 1.3 collective-permute-start.2
  22.8 1.3 collective-permute-start.3
  24.2 3.8 %collective-permute-done.3 = bf16[1,1024,128]{2,1,0:T(8,128)(2,1)S(1)} collective-permute-done((bf16[1,1024,128]{2,1,0:T(8,128)(2,1)S(1)}, bf16[1,1024,128]{2,1,0:T(8,128)(2,1)S(1)}, u32[]{:S(2)}, u32[]{:S(2)}) %collective-permute-start.3) | collective-permute-done | bytes 262176 | tf_op jit(solution)/shard_map/while/body/eval_jaxpr/ppermute | solution.py:17
  30.6 1.8 %conditional.6 = (bf16[1024,128]{1,0:T(8,128)(2,1)S(1)}, bf16[2,1024,128]{2,1,0:T(8,128)(2,1)S(1)}) conditional(s32[]{:T(128)} %convert_element_type.171, bf16[1024,128]{1,0:T(8,128)(2,1)S(1)} %select_select_fusion.4, (bf16[1024,128]{1,0:T(8,128)(2,1)S(1)}, bf16[4,128,128]{2,1,0:T(8,128)(2,1)}, f32[1024,4]{0,1:T(4,128)S(1)}) %tuple.102), branch_computations={%region_1.1_spmd, %region_2.2_spmd} | conditional | flops 135790592 | bytes 6963216 | solution.py:90
  30.7 1.6 %fusion.24 = (bf16[1024,4,128]{2,0,1:T(8,128)(2,1)S(1)}, f32[1024,4,128]{2,0,1:T(8,128)S(1)}) fusion(f32[1024,4]{0,1:T(4,128)S(1)} %get-tuple-element.394, bf16[4,128,128]{2,1,0:T(8,128)(2,1)} %get-tuple-element.393, bf16[1024,128]{1,0:T(8,128)(2,1)S(1)} %get-tuple-element.392), kind=kOutput, calls=%fused_computation.39 | convolution fusion | flops 135266304 | bytes 3555328 | tf_op jit(solution)/shard_map/while/body/eval_jaxpr/cond/branch_1_fun/ka,nab->knb/dot_general | solution.py:28
  32.5 1.8 %collective-permute-start = (bf16[1,1024,128]{2,1,0:T(8,128)(2,1)S(1)}, bf16[1,1024,128]{2,1,0:T(8,128)(2,1)S(1)}, u32[]{:S(2)}, u32[]{:S(2)}) collective-permute-start(bf16[1,1024,128]{2,1,0:T(8,128)(2,1)S(1)} %get-tuple-element.627), channel_id=1, source_target_pairs={{1,0},{2,1},{3,2},{0,3},{5,4},{6,5},{7,6},{4,7},{9,8},{10,9},{11,1... | collective-permute-start | bytes 786440 | tf_op jit(solution)/shard_map/while/body/eval_jaxpr/ppermute | solution.py:17
  34.6 4.3 %collective-permute-done = bf16[1,1024,128]{2,1,0:T(8,128)(2,1)S(1)} collective-permute-done((bf16[1,1024,128]{2,1,0:T(8,128)(2,1)S(1)}, bf16[1,1024,128]{2,1,0:T(8,128)(2,1)S(1)}, u32[]{:S(2)}, u32[]{:S(2)}) %collective-permute-start) | collective-permute-done | bytes 262176 | tf_op jit(solution)/shard_map/while/body/eval_jaxpr/ppermute | solution.py:17
  38.9 6.0 %collective-permute-done.1 = bf16[1,1024,128]{2,1,0:T(8,128)(2,1)S(1)} collective-permute-done((bf16[1,1024,128]{2,1,0:T(8,128)(2,1)S(1)}, bf16[1,1024,128]{2,1,0:T(8,128)(2,1)S(1)}, u32[]{:S(2)}, u32[]{:S(2)}) %collective-permute-start.1) | collective-permute-done | bytes 262176 | tf_op jit(solution)/shard_map/while/body/eval_jaxpr/ppermute | solution.py:14
  45.1 5.0 %collective-permute-start.2 = (bf16[1,1024,128]{2,1,0:T(8,128)(2,1)S(1)}, bf16[1,1024,128]{2,1,0:T(8,128)(2,1)S(1)}, u32[]{:S(2)}, u32[]{:S(2)}) collective-permute-start(bf16[1,1024,128]{2,1,0:T(8,128)(2,1)S(1)} %bitcast.59), channel_id=1, source_target_pairs={{0,4},{4,8},{8,12},{12,16},{16,20},{20,24},{24,28},{1,5},{5,9},{9,... | collective-permute-start | bytes 786440 | tf_op jit(solution)/shard_map/while/body/eval_jaxpr/ppermute | solution.py:14
  50.1 1.3 collective-permute-start.3
  51.4 4.1 %collective-permute-done.3 = bf16[1,1024,128]{2,1,0:T(8,128)(2,1)S(1)} collective-permute-done((bf16[1,1024,128]{2,1,0:T(8,128)(2,1)S(1)}, bf16[1,1024,128]{2,1,0:T(8,128)(2,1)S(1)}, u32[]{:S(2)}, u32[]{:S(2)}) %collective-permute-start.3) | collective-permute-done | bytes 262176 | tf_op jit(solution)/shard_map/while/body/eval_jaxpr/ppermute | solution.py:17
  58.2 1.8 %conditional.6 = (bf16[1024,128]{1,0:T(8,128)(2,1)S(1)}, bf16[2,1024,128]{2,1,0:T(8,128)(2,1)S(1)}) conditional(s32[]{:T(128)} %convert_element_type.171, bf16[1024,128]{1,0:T(8,128)(2,1)S(1)} %select_select_fusion.4, (bf16[1024,128]{1,0:T(8,128)(2,1)S(1)}, bf16[4,128,128]{2,1,0:T(8,128)(2,1)}, f32[1024,4]{0,1:T(4,128)S(1)}) %tuple.102), branch_computations={%region_1.1_spmd, %region_2.2_spmd} | conditional | flops 135790592 | bytes 6963216 | solution.py:90
  58.2 1.6 %fusion.24 = (bf16[1024,4,128]{2,0,1:T(8,128)(2,1)S(1)}, f32[1024,4,128]{2,0,1:T(8,128)S(1)}) fusion(f32[1024,4]{0,1:T(4,128)S(1)} %get-tuple-element.394, bf16[4,128,128]{2,1,0:T(8,128)(2,1)} %get-tuple-element.393, bf16[1024,128]{1,0:T(8,128)(2,1)S(1)} %get-tuple-element.392), kind=kOutput, calls=%fused_computation.39 | convolution fusion | flops 135266304 | bytes 3555328 | tf_op jit(solution)/shard_map/while/body/eval_jaxpr/cond/branch_1_fun/ka,nab->knb/dot_general | solution.py:28
  60.1 2.8 %collective-permute-start = (bf16[1,1024,128]{2,1,0:T(8,128)(2,1)S(1)}, bf16[1,1024,128]{2,1,0:T(8,128)(2,1)S(1)}, u32[]{:S(2)}, u32[]{:S(2)}) collective-permute-start(bf16[1,1024,128]{2,1,0:T(8,128)(2,1)S(1)} %get-tuple-element.627), channel_id=1, source_target_pairs={{1,0},{2,1},{3,2},{0,3},{5,4},{6,5},{7,6},{4,7},{9,8},{10,9},{11,1... | collective-permute-start | bytes 786440 | tf_op jit(solution)/shard_map/while/body/eval_jaxpr/ppermute | solution.py:17
  62.9 3.9 %collective-permute-done = bf16[1,1024,128]{2,1,0:T(8,128)(2,1)S(1)} collective-permute-done((bf16[1,1024,128]{2,1,0:T(8,128)(2,1)S(1)}, bf16[1,1024,128]{2,1,0:T(8,128)(2,1)S(1)}, u32[]{:S(2)}, u32[]{:S(2)}) %collective-permute-start) | collective-permute-done | bytes 262176 | tf_op jit(solution)/shard_map/while/body/eval_jaxpr/ppermute | solution.py:17
  66.8 6.9 %collective-permute-done.1 = bf16[1,1024,128]{2,1,0:T(8,128)(2,1)S(1)} collective-permute-done((bf16[1,1024,128]{2,1,0:T(8,128)(2,1)S(1)}, bf16[1,1024,128]{2,1,0:T(8,128)(2,1)S(1)}, u32[]{:S(2)}, u32[]{:S(2)}) %collective-permute-start.1) | collective-permute-done | bytes 262176 | tf_op jit(solution)/shard_map/while/body/eval_jaxpr/ppermute | solution.py:14
  73.8 6.4 %collective-permute-start.2 = (bf16[1,1024,128]{2,1,0:T(8,128)(2,1)S(1)}, bf16[1,1024,128]{2,1,0:T(8,128)(2,1)S(1)}, u32[]{:S(2)}, u32[]{:S(2)}) collective-permute-start(bf16[1,1024,128]{2,1,0:T(8,128)(2,1)S(1)} %bitcast.59), channel_id=1, source_target_pairs={{0,4},{4,8},{8,12},{12,16},{16,20},{20,24},{24,28},{1,5},{5,9},{9,... | collective-permute-start | bytes 786440 | tf_op jit(solution)/shard_map/while/body/eval_jaxpr/ppermute | solution.py:14
  81.5 5.4 %collective-permute-done.3 = bf16[1,1024,128]{2,1,0:T(8,128)(2,1)S(1)} collective-permute-done((bf16[1,1024,128]{2,1,0:T(8,128)(2,1)S(1)}, bf16[1,1024,128]{2,1,0:T(8,128)(2,1)S(1)}, u32[]{:S(2)}, u32[]{:S(2)}) %collective-permute-start.3) | collective-permute-done | bytes 262176 | tf_op jit(solution)/shard_map/while/body/eval_jaxpr/ppermute | solution.py:17
  89.6 1.8 %conditional.6 = (bf16[1024,128]{1,0:T(8,128)(2,1)S(1)}, bf16[2,1024,128]{2,1,0:T(8,128)(2,1)S(1)}) conditional(s32[]{:T(128)} %convert_element_type.171, bf16[1024,128]{1,0:T(8,128)(2,1)S(1)} %select_select_fusion.4, (bf16[1024,128]{1,0:T(8,128)(2,1)S(1)}, bf16[4,128,128]{2,1,0:T(8,128)(2,1)}, f32[1024,4]{0,1:T(4,128)S(1)}) %tuple.102), branch_computations={%region_1.1_spmd, %region_2.2_spmd} | conditional | flops 135790592 | bytes 6963216 | solution.py:90
  89.7 1.6 %fusion.24 = (bf16[1024,4,128]{2,0,1:T(8,128)(2,1)S(1)}, f32[1024,4,128]{2,0,1:T(8,128)S(1)}) fusion(f32[1024,4]{0,1:T(4,128)S(1)} %get-tuple-element.394, bf16[4,128,128]{2,1,0:T(8,128)(2,1)} %get-tuple-element.393, bf16[1024,128]{1,0:T(8,128)(2,1)S(1)} %get-tuple-element.392), kind=kOutput, calls=%fused_computation.39 | convolution fusion | flops 135266304 | bytes 3555328 | tf_op jit(solution)/shard_map/while/body/eval_jaxpr/cond/branch_1_fun/ka,nab->knb/dot_general | solution.py:28
  91.5 3.4 %collective-permute-start = (bf16[1,1024,128]{2,1,0:T(8,128)(2,1)S(1)}, bf16[1,1024,128]{2,1,0:T(8,128)(2,1)S(1)}, u32[]{:S(2)}, u32[]{:S(2)}) collective-permute-start(bf16[1,1024,128]{2,1,0:T(8,128)(2,1)S(1)} %get-tuple-element.627), channel_id=1, source_target_pairs={{1,0},{2,1},{3,2},{0,3},{5,4},{6,5},{7,6},{4,7},{9,8},{10,9},{11,1... | collective-permute-start | bytes 786440 | tf_op jit(solution)/shard_map/while/body/eval_jaxpr/ppermute | solution.py:17
  94.9 3.9 %collective-permute-done = bf16[1,1024,128]{2,1,0:T(8,128)(2,1)S(1)} collective-permute-done((bf16[1,1024,128]{2,1,0:T(8,128)(2,1)S(1)}, bf16[1,1024,128]{2,1,0:T(8,128)(2,1)S(1)}, u32[]{:S(2)}, u32[]{:S(2)}) %collective-permute-start) | collective-permute-done | bytes 262176 | tf_op jit(solution)/shard_map/while/body/eval_jaxpr/ppermute | solution.py:17
  98.8 6.4 %collective-permute-done.1 = bf16[1,1024,128]{2,1,0:T(8,128)(2,1)S(1)} collective-permute-done((bf16[1,1024,128]{2,1,0:T(8,128)(2,1)S(1)}, bf16[1,1024,128]{2,1,0:T(8,128)(2,1)S(1)}, u32[]{:S(2)}, u32[]{:S(2)}) %collective-permute-start.1) | collective-permute-done | bytes 262176 | tf_op jit(solution)/shard_map/while/body/eval_jaxpr/ppermute | solution.py:14
  105.3 5.2 %collective-permute-start.2 = (bf16[1,1024,128]{2,1,0:T(8,128)(2,1)S(1)}, bf16[1,1024,128]{2,1,0:T(8,128)(2,1)S(1)}, u32[]{:S(2)}, u32[]{:S(2)}) collective-permute-start(bf16[1,1024,128]{2,1,0:T(8,128)(2,1)S(1)} %bitcast.59), channel_id=1, source_target_pairs={{0,4},{4,8},{8,12},{12,16},{16,20},{20,24},{24,28},{1,5},{5,9},{9,... | collective-permute-start | bytes 786440 | tf_op jit(solution)/shard_map/while/body/eval_jaxpr/ppermute | solution.py:14
  111.9 5.0 %collective-permute-done.3 = bf16[1,1024,128]{2,1,0:T(8,128)(2,1)S(1)} collective-permute-done((bf16[1,1024,128]{2,1,0:T(8,128)(2,1)S(1)}, bf16[1,1024,128]{2,1,0:T(8,128)(2,1)S(1)}, u32[]{:S(2)}, u32[]{:S(2)}) %collective-permute-start.3) | collective-permute-done | bytes 262176 | tf_op jit(solution)/shard_map/while/body/eval_jaxpr/ppermute | solution.py:17
  117.3 43.5 %psum.7 = f32[1024]{0:T(1024)} all-reduce(f32[1024]{0:T(1024)S(1)} %get-tuple-element.425), channel_id=1, replica_groups=mesh['seg'=8,'sec'=4] {'seg','sec'}, use_global_device_ids=true, to_apply=%region_9.10 | all-reduce | flops 1024 | bytes 8192 | tf_op jit(solution)/shard_map/psum | solution.py:123
  (68 shorter events, 15.1 us)
Async XLA Ops:
  4.2 11.8 %collective-permute-start = (bf16[1,1024,128]{2,1,0:T(8,128)(2,1)S(1)}, bf16[1,1024,128]{2,1,0:T(8,128)(2,1)S(1)}, u32[]{:S(2)}, u32[]{:S(2)}) collective-permute-start(bf16[1,1024,128]{2,1,0:T(8,128)(2,1)S(1)} %get-tuple-element.627), channel_id=1, source_target_pairs={{1,0},{2,1},{3,2},{0,3},{5,4},{6,5},{7,6},{4,7},{9,8},{10,9},{11,1... | collective-permute-start | bytes 786440 | tf_op jit(solution)/shard_map/while/body/eval_jaxpr/ppermute | solution.py:17
  9.3 12.1 %collective-permute-start.1 = (bf16[1,1024,128]{2,1,0:T(8,128)(2,1)S(1)}, bf16[1,1024,128]{2,1,0:T(8,128)(2,1)S(1)}, u32[]{:S(2)}, u32[]{:S(2)}) collective-permute-start(bf16[1,1024,128]{2,1,0:T(8,128)(2,1)S(1)} %get-tuple-element.628), channel_id=1, source_target_pairs={{0,1},{1,2},{2,3},{3,0},{4,5},{5,6},{6,7},{7,4},{8,9},{9,10},{10,1... | collective-permute-start | bytes 786440 | tf_op jit(solution)/shard_map/while/body/eval_jaxpr/ppermute | solution.py:14
  21.5 2.7 %collective-permute-start.2 = (bf16[1,1024,128]{2,1,0:T(8,128)(2,1)S(1)}, bf16[1,1024,128]{2,1,0:T(8,128)(2,1)S(1)}, u32[]{:S(2)}, u32[]{:S(2)}) collective-permute-start(bf16[1,1024,128]{2,1,0:T(8,128)(2,1)S(1)} %bitcast.59), channel_id=1, source_target_pairs={{0,4},{4,8},{8,12},{12,16},{16,20},{20,24},{24,28},{1,5},{5,9},{9,... | collective-permute-start | bytes 786440 | tf_op jit(solution)/shard_map/while/body/eval_jaxpr/ppermute | solution.py:14
  22.8 5.1 %collective-permute-start.3 = (bf16[1,1024,128]{2,1,0:T(8,128)(2,1)S(1)}, bf16[1,1024,128]{2,1,0:T(8,128)(2,1)S(1)}, u32[]{:S(2)}, u32[]{:S(2)}) collective-permute-start(bf16[1,1024,128]{2,1,0:T(8,128)(2,1)S(1)} %bitcast.60), channel_id=1, source_target_pairs={{4,0},{8,4},{12,8},{16,12},{20,16},{24,20},{28,24},{5,1},{9,5},{13... | collective-permute-start | bytes 786440 | tf_op jit(solution)/shard_map/while/body/eval_jaxpr/ppermute | solution.py:17
  32.5 6.4 %collective-permute-start = (bf16[1,1024,128]{2,1,0:T(8,128)(2,1)S(1)}, bf16[1,1024,128]{2,1,0:T(8,128)(2,1)S(1)}, u32[]{:S(2)}, u32[]{:S(2)}) collective-permute-start(bf16[1,1024,128]{2,1,0:T(8,128)(2,1)S(1)} %get-tuple-element.627), channel_id=1, source_target_pairs={{1,0},{2,1},{3,2},{0,3},{5,4},{6,5},{7,6},{4,7},{9,8},{10,9},{11,1... | collective-permute-start | bytes 786440 | tf_op jit(solution)/shard_map/while/body/eval_jaxpr/ppermute | solution.py:17
  34.3 10.7 %collective-permute-start.1 = (bf16[1,1024,128]{2,1,0:T(8,128)(2,1)S(1)}, bf16[1,1024,128]{2,1,0:T(8,128)(2,1)S(1)}, u32[]{:S(2)}, u32[]{:S(2)}) collective-permute-start(bf16[1,1024,128]{2,1,0:T(8,128)(2,1)S(1)} %get-tuple-element.628), channel_id=1, source_target_pairs={{0,1},{1,2},{2,3},{3,0},{4,5},{5,6},{6,7},{7,4},{8,9},{9,10},{10,1... | collective-permute-start | bytes 786440 | tf_op jit(solution)/shard_map/while/body/eval_jaxpr/ppermute | solution.py:14
  45.1 6.3 %collective-permute-start.2 = (bf16[1,1024,128]{2,1,0:T(8,128)(2,1)S(1)}, bf16[1,1024,128]{2,1,0:T(8,128)(2,1)S(1)}, u32[]{:S(2)}, u32[]{:S(2)}) collective-permute-start(bf16[1,1024,128]{2,1,0:T(8,128)(2,1)S(1)} %bitcast.59), channel_id=1, source_target_pairs={{0,4},{4,8},{8,12},{12,16},{16,20},{20,24},{24,28},{1,5},{5,9},{9,... | collective-permute-start | bytes 786440 | tf_op jit(solution)/shard_map/while/body/eval_jaxpr/ppermute | solution.py:14
  50.1 5.5 %collective-permute-start.3 = (bf16[1,1024,128]{2,1,0:T(8,128)(2,1)S(1)}, bf16[1,1024,128]{2,1,0:T(8,128)(2,1)S(1)}, u32[]{:S(2)}, u32[]{:S(2)}) collective-permute-start(bf16[1,1024,128]{2,1,0:T(8,128)(2,1)S(1)} %bitcast.60), channel_id=1, source_target_pairs={{4,0},{8,4},{12,8},{16,12},{20,16},{24,20},{28,24},{5,1},{9,5},{13... | collective-permute-start | bytes 786440 | tf_op jit(solution)/shard_map/while/body/eval_jaxpr/ppermute | solution.py:17
  60.1 6.7 %collective-permute-start = (bf16[1,1024,128]{2,1,0:T(8,128)(2,1)S(1)}, bf16[1,1024,128]{2,1,0:T(8,128)(2,1)S(1)}, u32[]{:S(2)}, u32[]{:S(2)}) collective-permute-start(bf16[1,1024,128]{2,1,0:T(8,128)(2,1)S(1)} %get-tuple-element.627), channel_id=1, source_target_pairs={{1,0},{2,1},{3,2},{0,3},{5,4},{6,5},{7,6},{4,7},{9,8},{10,9},{11,1... | collective-permute-start | bytes 786440 | tf_op jit(solution)/shard_map/while/body/eval_jaxpr/ppermute | solution.py:17
  62.9 10.8 %collective-permute-start.1 = (bf16[1,1024,128]{2,1,0:T(8,128)(2,1)S(1)}, bf16[1,1024,128]{2,1,0:T(8,128)(2,1)S(1)}, u32[]{:S(2)}, u32[]{:S(2)}) collective-permute-start(bf16[1,1024,128]{2,1,0:T(8,128)(2,1)S(1)} %get-tuple-element.628), channel_id=1, source_target_pairs={{0,1},{1,2},{2,3},{3,0},{4,5},{5,6},{6,7},{7,4},{8,9},{9,10},{10,1... | collective-permute-start | bytes 786440 | tf_op jit(solution)/shard_map/while/body/eval_jaxpr/ppermute | solution.py:14
  73.8 7.7 %collective-permute-start.2 = (bf16[1,1024,128]{2,1,0:T(8,128)(2,1)S(1)}, bf16[1,1024,128]{2,1,0:T(8,128)(2,1)S(1)}, u32[]{:S(2)}, u32[]{:S(2)}) collective-permute-start(bf16[1,1024,128]{2,1,0:T(8,128)(2,1)S(1)} %bitcast.59), channel_id=1, source_target_pairs={{0,4},{4,8},{8,12},{12,16},{16,20},{20,24},{24,28},{1,5},{5,9},{9,... | collective-permute-start | bytes 786440 | tf_op jit(solution)/shard_map/while/body/eval_jaxpr/ppermute | solution.py:14
  80.2 6.8 %collective-permute-start.3 = (bf16[1,1024,128]{2,1,0:T(8,128)(2,1)S(1)}, bf16[1,1024,128]{2,1,0:T(8,128)(2,1)S(1)}, u32[]{:S(2)}, u32[]{:S(2)}) collective-permute-start(bf16[1,1024,128]{2,1,0:T(8,128)(2,1)S(1)} %bitcast.60), channel_id=1, source_target_pairs={{4,0},{8,4},{12,8},{16,12},{20,16},{24,20},{28,24},{5,1},{9,5},{13... | collective-permute-start | bytes 786440 | tf_op jit(solution)/shard_map/while/body/eval_jaxpr/ppermute | solution.py:17
  91.5 7.3 %collective-permute-start = (bf16[1,1024,128]{2,1,0:T(8,128)(2,1)S(1)}, bf16[1,1024,128]{2,1,0:T(8,128)(2,1)S(1)}, u32[]{:S(2)}, u32[]{:S(2)}) collective-permute-start(bf16[1,1024,128]{2,1,0:T(8,128)(2,1)S(1)} %get-tuple-element.627), channel_id=1, source_target_pairs={{1,0},{2,1},{3,2},{0,3},{5,4},{6,5},{7,6},{4,7},{9,8},{10,9},{11,1... | collective-permute-start | bytes 786440 | tf_op jit(solution)/shard_map/while/body/eval_jaxpr/ppermute | solution.py:17
  94.9 10.3 %collective-permute-start.1 = (bf16[1,1024,128]{2,1,0:T(8,128)(2,1)S(1)}, bf16[1,1024,128]{2,1,0:T(8,128)(2,1)S(1)}, u32[]{:S(2)}, u32[]{:S(2)}) collective-permute-start(bf16[1,1024,128]{2,1,0:T(8,128)(2,1)S(1)} %get-tuple-element.628), channel_id=1, source_target_pairs={{0,1},{1,2},{2,3},{3,0},{4,5},{5,6},{6,7},{7,4},{8,9},{9,10},{10,1... | collective-permute-start | bytes 786440 | tf_op jit(solution)/shard_map/while/body/eval_jaxpr/ppermute | solution.py:14
  105.3 6.5 %collective-permute-start.2 = (bf16[1,1024,128]{2,1,0:T(8,128)(2,1)S(1)}, bf16[1,1024,128]{2,1,0:T(8,128)(2,1)S(1)}, u32[]{:S(2)}, u32[]{:S(2)}) collective-permute-start(bf16[1,1024,128]{2,1,0:T(8,128)(2,1)S(1)} %bitcast.59), channel_id=1, source_target_pairs={{0,4},{4,8},{8,12},{12,16},{16,20},{20,24},{24,28},{1,5},{5,9},{9,... | collective-permute-start | bytes 786440 | tf_op jit(solution)/shard_map/while/body/eval_jaxpr/ppermute | solution.py:14
  110.5 6.3 %collective-permute-start.3 = (bf16[1,1024,128]{2,1,0:T(8,128)(2,1)S(1)}, bf16[1,1024,128]{2,1,0:T(8,128)(2,1)S(1)}, u32[]{:S(2)}, u32[]{:S(2)}) collective-permute-start(bf16[1,1024,128]{2,1,0:T(8,128)(2,1)S(1)} %bitcast.60), channel_id=1, source_target_pairs={{4,0},{8,4},{12,8},{16,12},{20,16},{24,20},{28,24},{5,1},{9,5},{13... | collective-permute-start | bytes 786440 | tf_op jit(solution)/shard_map/while/body/eval_jaxpr/ppermute | solution.py:17
where the time goes:
time: 162 us; the launch traced here: 161 us
  waiting for transfers between devices  61.9 us (38%)
  blocking collectives  43.5 us (27%)
  starting transfers between devices  36.4 us (22%)
  other arithmetic  11.5 us (7%)
  matrix products  6.5 us (4%)
    psum x1, blocking collectives, per_device(): return lax.psum(final_state[1], ('seg', 'sec'))  43.5 us
    ppermute x8, waiting for transfers between devices, padded_2(): lax.ppermute(lax.slice_in_dim(block, 0, width, axis=dim), axis, backward)  37.2 us
    ppermute x8, waiting for transfers between devices, padded_2(): lax.ppermute(lax.slice_in_dim(block, block.shape[dim] - width, None, axis...  24.7 us
    ppermute x8, starting transfers between devices, padded_2(): lax.ppermute(lax.slice_in_dim(block, 0, width, axis=dim), axis, backward)  18.2 us
    ppermute x8, starting transfers between devices, padded_2(): lax.ppermute(lax.slice_in_dim(block, block.shape[dim] - width, None, axis...  18.1 us
    dot_general x4, matrix products, forward_send(): jnp.einsum('ka,nab->knb', vector, block_site, preferred_element_type=jnp....  6.5 us
    select_n x4, other arithmetic, section(): vector = jnp.where(is_first, initial(), incoming)  3.5 us
  transfers between devices with their start and end apart: 16, of which 12 were waited for; matrix products, arithmetic and copies ran while one was open for 0% of the time, Pallas kernels for 0%

commit v1 on v0

--- a/solution.py
+++ b/solution.py
@@ -1,7 +1,332 @@
+import functools
+
 import jax
 import jax.numpy as jnp
 from jax import lax
+from jax.experimental import pallas as pl
+from jax.experimental.pallas import tpu as pltpu
 from jax.sharding import PartitionSpec as P
+
+MESH = pl.DeviceIdType.MESH
+SLOTS = (0, 3, 1, 2)
+
+
+def tree_kernel(
+    seg_count, sec_count,
+    blocks_hbm, left_ref, right_ref, occ_ref, start_ref, out_ref,
+    mats, x_in, y_out, big_out, l_in, r_in, occ_in, one_l, one_r, sel_r, fin,
+    mat_sem, ch_send, ch_recv, l_recv, occ_send, occ_recv, fin_send, fin_recv,
+):
+    seg = lax.axis_index("seg")
+    sec = lax.axis_index("sec")
+    up = lax.rem(sec + 1, sec_count)
+    down = lax.rem(sec + sec_count - 1, sec_count)
+    half = seg_count // 2
+    last = seg_count - 1
+    near = (sec, up, down)
+    hub = half
+
+    load = pltpu.make_async_copy(blocks_hbm, mats, mat_sem)
+    load.start()
+
+    barrier = pltpu.get_barrier_semaphore()
+
+    def greet(seg_to, sec_to):
+        pl.semaphore_signal(barrier, inc=1, device_id=(seg_to, sec_to), device_id_type=MESH)
+
+    @pl.when(seg == hub)
+    def _():
+        for i in range(seg_count):
+            if i != hub:
+                greet(i, sec)
+        for i in (hub - 1, hub + 1):
+            greet(i, up)
+            greet(i, down)
+        for step in range(1, sec_count):
+            greet(hub, lax.rem(sec + step, sec_count))
+
+    @pl.when(seg != hub)
+    def _():
+        @pl.when(jnp.logical_and(seg >= 1, seg < last))
+        def _():
+            before = jnp.where(seg < half, seg - 1, seg + 1)
+            for place in near:
+                greet(before, place)
+
+        @pl.when(seg == last)
+        def _():
+            greet(last, up)
+            greet(last, down)
+
+        for place in range(sec_count):
+            greet(hub, place)
+
+    def send(src, dst, send_sem, recv_sem, seg_to, sec_to):
+        copy = pltpu.make_async_remote_copy(
+            src_ref=src, dst_ref=dst, send_sem=send_sem, recv_sem=recv_sem,
+            device_id=(seg_to, sec_to), device_id_type=MESH,
+        )
+        copy.start()
+        return copy
+
+    def arrived(dst, recv_sem):
+        pltpu.make_async_remote_copy(
+            src_ref=dst, dst_ref=dst, send_sem=ch_send.at[0], recv_sem=recv_sem,
+            device_id=(seg, sec), device_id_type=MESH,
+        ).wait_recv()
+
+    def send_occ():
+        return send(occ_ref, occ_in.at[seg], occ_send, occ_recv.at[seg], hub, sec)
+
+    rows16 = lax.broadcasted_iota(jnp.int32, (16, 128), 0)
+
+    def pick(index, parts):
+        total = parts[3]
+        for n in (2, 1, 0):
+            total = jnp.where(index == n, parts[n], total)
+        return total
+
+    def left_products(x):
+        return [
+            jnp.dot(x, mats[n], preferred_element_type=jnp.float32).astype(jnp.bfloat16)
+            for n in SLOTS
+        ]
+
+    def left_send(out, into, sems):
+        return (
+            send(out.at[0:2], into.at[0:2], ch_send.at[0], sems.at[0], seg + 1, sec),
+            send(out.at[2:3], into.at[2:3], ch_send.at[1], sems.at[1], seg + 1, up),
+            send(out.at[3:4], into.at[3:4], ch_send.at[2], sems.at[2], seg + 1, down),
+        )
+
+    def left_wait(into, sems):
+        arrived(into.at[0:2], sems.at[0])
+        arrived(into.at[2:3], sems.at[1])
+        arrived(into.at[3:4], sems.at[2])
+
+    def left_slots():
+        by_n = [None] * 4
+        for place, n in enumerate(SLOTS):
+            by_n[n] = x_in[place]
+        return by_n
+
+    def f32(parts):
+        return [part.astype(jnp.float32) for part in parts]
+
+    def right_products(parts):
+        return [
+            lax.dot_general(
+                parts[place], mats[n], (((1,), (1,)), ((), ())),
+                preferred_element_type=jnp.float32,
+            )
+            for n, place in enumerate((0, 1, 2, 0))
+        ]
+
+    def right_send(out, into):
+        return (
+            send(out, into.at[0], ch_send.at[0], ch_recv.at[0], seg - 1, sec),
+            send(out, into.at[2], ch_send.at[1], ch_recv.at[2], seg - 1, up),
+            send(out, into.at[1], ch_send.at[2], ch_recv.at[1], seg - 1, down),
+        )
+
+    def right_wait(into):
+        for place in range(3):
+            arrived(into.at[place], ch_recv.at[place])
+
+    def finish(copies):
+        for copy in copies:
+            copy.wait_send()
+
+    def edge_rows(ref):
+        return jnp.broadcast_to(ref[...].astype(jnp.float32), (16, 128)).astype(jnp.bfloat16)
+
+    @pl.when(seg == 0)
+    def _():
+        pl.semaphore_wait(barrier, 4)
+        load.wait()
+        for place, part in enumerate(left_products(edge_rows(left_ref))):
+            y_out[place] = part
+        copies = left_send(y_out, x_in, ch_recv)
+        occ = send_occ()
+        finish(copies + (occ,))
+
+    @pl.when(jnp.logical_or(seg == 1, seg == 2))
+    def _():
+        pl.semaphore_wait(barrier, 4)
+        occ = send_occ()
+        load.wait()
+        left_wait(x_in, ch_recv)
+        index = jnp.where(seg == 1, lax.rem(rows16, 4), lax.div(rows16, 4))
+        x = pick(index, f32(left_slots())).astype(jnp.bfloat16)
+        for place, part in enumerate(left_products(x)):
+            y_out[place] = part
+        copies = left_send(y_out, x_in, ch_recv)
+        finish(copies + (occ,))
+
+    @pl.when(seg == 3)
+    def _():
+        pl.semaphore_wait(barrier, 3)
+        occ = send_occ()
+        load.wait()
+        left_wait(x_in, ch_recv)
+        x = jnp.concatenate(left_slots(), axis=0)
+        for place, part in enumerate(left_products(x)):
+            big_out[place] = part
+        copies = left_send(big_out, l_in, l_recv)
+        finish(copies + (occ,))
+
+    @pl.when(seg == last)
+    def _():
+        own = edge_rows(right_ref)
+        y_out[0] = own
+        pl.semaphore_wait(barrier, 6)
+        edges = (
+            send(y_out.at[0], x_in.at[2], ch_send.at[0], ch_recv.at[2], seg, up),
+            send(y_out.at[0], x_in.at[1], ch_send.at[1], ch_recv.at[1], seg, down),
+        )
+        occ = send_occ()
+        load.wait()
+        arrived(x_in.at[1], ch_recv.at[1])
+        arrived(x_in.at[2], ch_recv.at[2])
+        parts = right_products((own, x_in[1], x_in[2]))
+        y_out[1] = pick(lax.rem(rows16, 4), parts).astype(jnp.bfloat16)
+        finish(edges)
+        copies = right_send(y_out.at[1], x_in)
+        finish(copies + (occ,))
+
+    @pl.when(seg == 6)
+    def _():
+        pl.semaphore_wait(barrier, 4)
+        occ = send_occ()
+        load.wait()
+        right_wait(x_in)
+        parts = right_products((x_in[0], x_in[1], x_in[2]))
+        y_out[0] = pick(lax.div(rows16, 4), parts).astype(jnp.bfloat16)
+        copies = right_send(y_out.at[0], x_in)
+        finish(copies + (occ,))
+
+    @pl.when(seg == 5)
+    def _():
+        pl.semaphore_wait(barrier, 3)
+        occ = send_occ()
+        load.wait()
+        right_wait(x_in)
+        parts = right_products((x_in[0], x_in[1], x_in[2]))
+        for n in range(4):
+            big_out[0, n * 16:(n + 1) * 16, :] = parts[n].astype(jnp.bfloat16)
+        copies = right_send(big_out.at[0], r_in)
+        finish(copies + (occ,))
+
+    @pl.when(seg == hub)
+    def _():
+        for i in range(seg_count):
+            if i != hub:
+                arrived(occ_in.at[i], occ_recv.at[i])
+        occ = [occ_ref[...] if i == hub else occ_in[i] for i in range(seg_count)]
+        middle = start_ref[...]
+        for n in occ[:half]:
+            middle = middle + jnp.where(n == 1, 1, 0) - jnp.where(n == 2, 1, 0)
+        slot = jnp.where(occ[3] == 0, 0, jnp.where(occ[3] == 3, 1, occ[3] + 1))
+        key_l = slot * 64 + occ[2] * 16 + occ[1] * 4 + occ[0]
+        key_l = jnp.where(lax.rem(middle + 2 * sec_count, sec_count) == sec, key_l, -1)
+        key_r = occ[4] * 64 + occ[5] * 16 + occ[6] * 4 + occ[7]
+        rows = lax.broadcasted_iota(jnp.int32, (256, 128), 0)
+        for j in range(8):
+            here = slice(j * 128, (j + 1) * 128)
+            one_r[:, here] = jnp.where(rows == key_r[j:j + 1, :], 1.0, 0.0).astype(jnp.bfloat16)
+            one_l[:, here] = jnp.where(rows == key_l[j:j + 1, :], 1.0, 0.0).astype(jnp.bfloat16)
+        load.wait()
+
+        def select(vectors, one_hot):
+            return lax.dot_general(
+                vectors, one_hot[...], (((0,), (0,)), ((), ())),
+                preferred_element_type=jnp.float32,
+            )
+
+        right_wait(r_in)
+        parts = right_products((r_in[0], r_in[1], r_in[2]))
+        right = jnp.concatenate([part.astype(jnp.bfloat16) for part in parts], axis=0)
+        sel_r[...] = select(right, one_r)
+        left_wait(l_in, l_recv)
+        left = jnp.concatenate([l_in[place] for place in range(4)], axis=0)
+        value = jnp.sum(select(left, one_l) * sel_r[...], axis=0, keepdims=True)
+        for j in range(8):
+            fin[sec, j:j + 1, :] = value[:, j * 128:(j + 1) * 128]
+        count = seg_count * sec_count
+        pl.semaphore_wait(barrier, count - 1)
+        me = seg * sec_count + sec
+        copies = []
+        for step in range(1, count):
+            to = lax.rem(me + step, count)
+            copies.append(
+                send(
+                    fin.at[sec], fin.at[sec], fin_send.at[step - 1], fin_recv.at[sec],
+                    lax.div(to, sec_count), lax.rem(to, sec_count),
+                )
+            )
+        finish(copies)
+
+    for place in range(sec_count):
+        @pl.when(jnp.logical_or(seg != hub, sec != place))
+        def _():
+            arrived(fin.at[place], fin_recv.at[place])
+
+    out_ref[...] = (fin[0] + fin[1]) + (fin[2] + fin[3])
+
+
+def tree_device(blocks, left_edge, right_edge, occupation, start_sector):
+    seg_count = lax.axis_size("seg")
+    sec_count = lax.axis_size("sec")
+    vmem = pl.BlockSpec(memory_space=pltpu.VMEM)
+    dma = pltpu.SemaphoreType.DMA
+    bf16, f32, i32 = jnp.bfloat16, jnp.float32, jnp.int32
+    values = pl.pallas_call(
+        functools.partial(tree_kernel, seg_count, sec_count),
+        out_shape=jax.ShapeDtypeStruct((8, 128), f32),
+        in_specs=[pl.BlockSpec(memory_space=pl.ANY)] + [vmem] * 4,
+        out_specs=vmem,
+        scratch_shapes=[
+            pltpu.VMEM((4, 128, 128), bf16),
+            pltpu.VMEM((4, 16, 128), bf16),
+            pltpu.VMEM((4, 16, 128), bf16),
+            pltpu.VMEM((4, 64, 128), bf16),
+            pltpu.VMEM((4, 64, 128), bf16),
+            pltpu.VMEM((3, 64, 128), bf16),
+            pltpu.VMEM((8, 8, 128), i32),
+            pltpu.VMEM((256, 1024), bf16),
+            pltpu.VMEM((256, 1024), bf16),
+            pltpu.VMEM((128, 1024), f32),
+            pltpu.VMEM((4, 8, 128), f32),
+            dma,
+            dma((3,)),
+            dma((3,)),
+            dma((3,)),
+            dma,
+            dma((8,)),
+            dma((seg_count * sec_count - 1,)),
+            dma((4,)),
+        ],
+        compiler_params=pltpu.CompilerParams(
+            collective_id=0, has_side_effects=True, vmem_limit_bytes=16 * 1024 * 1024
+        ),
+    )(
+        blocks.reshape(4, 128, 128),
+        left_edge,
+        right_edge,
+        occupation.reshape(8, 128),
+        start_sector.reshape(8, 128),
+    )
+    return values.reshape(1024)
+
+
+def fits_tree(mesh, blocks, occupation):
+    seg_count, sec_count = mesh.shape["seg"], mesh.shape["sec"]
+    return (
+        seg_count == 8
+        and sec_count == 4
+        and blocks.shape == (8, 4, 4, 128, 128)
+        and occupation.shape == (1024, 8)
+    )
 
 
 def padded_2(block, sides, width, periodic):
@@ -131,7 +456,11 @@
         P(None, "seg"),
         P(),
     )
-    out_specs = P()
-    return jax.shard_map(
-        per_device, mesh=mesh, in_specs=in_specs, out_specs=out_specs, check_vma=False
-    )
+
+    def run(blocks, left_edge, right_edge, occupation, start_sector):
+        body = tree_device if fits_tree(mesh, blocks, occupation) else per_device
+        return jax.shard_map(
+            body, mesh=mesh, in_specs=in_specs, out_specs=P(), check_vma=False
+        )(blocks, left_edge, right_edge, occupation, start_sector)
+
+    return run

time: 162 us -> 27.5 us (0.17)
  waiting for transfers between devices: 61.9 us -> 0 us
  blocking collectives: 43.5 us -> 0 us
  starting transfers between devices: 36.4 us -> 0 us
  Pallas kernels: 0 us -> 24.4 us
  other arithmetic: 11.5 us -> 0 us
  matrix products: 6.5 us -> 0 us
  local copies, waits for them, and re-layouts: 0.33 us -> 2.88 us
    ppermute x16 -> x0, waiting for transfers between devices: 61.9 us -> none  [the longest x8 37.2 us: padded_2(): lax.ppermute(lax.slice_in_dim(block, 0, width, axis=dim), axis, backward)]
    psum x1 -> x0, blocking collectives: 43.5 us -> none  [per_device(): return lax.psum(final_state[1], ('seg', 'sec'))]
    ppermute x16 -> x0, starting transfers between devices: 36.4 us -> none  [the longest x8 18.2 us: padded_2(): lax.ppermute(lax.slice_in_dim(block, 0, width, axis=dim), axis, backward)]
    pallas_call x0 -> x1, Pallas kernels: none -> 24.4 us  [tree_device(): pl.pallas_call(functools.partial(tree_kernel, seg_count, sec_count), out_...]
    dot_general x4 -> x0, matrix products: 6.5 us -> none  [forward_send(): jnp.einsum('ka,nab->knb', vector, block_site, preferred_element_type=jnp....]
    select_n x12 -> x0, other arithmetic: 3.65 us -> none  [the longest x4 3.5 us: section(): vector = jnp.where(is_first, initial(), incoming)]
    convert_element_type x16 -> x0, other arithmetic: 3.44 us -> none  [the longest x4 2.78 us: state_masks(): return (occ_site[:, None] == levels[None, :]).astype(jnp.float32)]
    unnamed x0 -> x11, local copies, waits for them, and re-layouts: none -> 2.88 us
  transfers between devices with their start and end apart: 16 -> 0, of which waited for: 12 -> 0; matrix products, arithmetic and copies ran while one was open for 0% -> 0% of each run, Pallas kernels for 0% -> 0%
where the time goes in v1:
time: 27.5 us; the launch traced here: 27.3 us
  Pallas kernels  24.4 us (89%)
  local copies, waits for them, and re-layouts  2.88 us (10%)
    pallas_call x1, Pallas kernels, tree_device(): pl.pallas_call(functools.partial(tree_kernel, seg_count, sec_count), out_...  24.4 us
    unnamed x11, local copies, waits for them, and re-layouts  2.88 us

profile of v1, /device:TPU:0, one launch (start us, length us, event | category | flops | bytes accessed | tf_op | source)
XLA Modules:
  0.0 27.3 jit_solution(17421267154696533491)
XLA Ops:
  0.0 0.0 copy-start.1
  0.0 0.0 copy-start.3
  0.0 0.0 copy-start.4
  0.0 0.7 %copy-done.1 = s32[1024,1]{0,1:T(1,128)S(1)} copy-done((s32[1024,1]{0,1:T(1,128)S(1)}, s32[1024,1]{0,1:T(1,128)}, u32[]{:S(2)}) %copy-start.1) | copy-done | bytes 4120
  0.7 0.0 copy-done.3
  0.7 0.0 copy-done.4
  0.7 0.0 copy-start
  0.7 0.9 %copy-done = bf16[1,4,1,128,128]{4,3,2,1,0:T(8,128)(2,1)S(1)} copy-done((bf16[1,4,1,128,128]{4,3,2,1,0:T(8,128)(2,1)S(1)}, bf16[1,4,1,128,128]{4,3,2,1,0:T(8,128)(2,1)}, u32[]{:S(2)}) %copy-start) | copy-done | bytes 131096
  1.6 0.0 copy-start.2
  1.6 0.7 %copy-done.2 = s32[1024]{0:T(1024)S(1)} copy-done((s32[1024]{0:T(1024)S(1)}, s32[1024]{0:T(1024)}, u32[]{:S(2)}) %copy-start.2) | copy-done | bytes 4120
  2.3 24.4 %shard_map.55 = f32[8,128]{1,0:T(8,128)S(1)} custom-call(bf16[4,128,128]{2,1,0:T(8,128)(2,1)S(1)} %bitcast.4, bf16[1,128]{1,0:T(2,128)(2,1)S(1)} %copy-done.3, bf16[1,128]{1,0:T(2,128)(2,1)S(1)} %copy-done.4, s32[8,128]{1,0:T(8,128)S(1)} %bitcast.6, s32[8,128]{1,0:T(8,128)S(1)} %bitcast.7), custom_call_target="tpu_custom_call" | custom-call | tf_op jit(solution)/shard_map/pallas_call | solution.py:283
  26.7 0.6 %copy.7 = f32[1024]{0:T(1024)} copy(f32[1024]{0:T(1024)S(1)} %bitcast.5) | data formatting | bytes 8192
Async XLA Ops:
  0.0 0.7 %copy-start.1 = (s32[1024,1]{0,1:T(1,128)S(1)}, s32[1024,1]{0,1:T(1,128)}, u32[]{:S(2)}) copy-start(s32[1024,1]{0,1:T(1,128)} %param.8) | copy-start | bytes 12292
  0.0 0.7 %copy-start.3 = (bf16[1,128]{1,0:T(2,128)(2,1)S(1)}, bf16[1,128]{1,0:T(2,128)(2,1)}, u32[]{:S(2)}) copy-start(bf16[1,128]{1,0:T(2,128)(2,1)} %left_ref.1) | copy-start | bytes 772
  0.0 0.7 %copy-start.4 = (bf16[1,128]{1,0:T(2,128)(2,1)S(1)}, bf16[1,128]{1,0:T(2,128)(2,1)}, u32[]{:S(2)}) copy-start(bf16[1,128]{1,0:T(2,128)(2,1)} %right_ref.1) | copy-start | bytes 772
  0.7 0.9 %copy-start = (bf16[1,4,1,128,128]{4,3,2,1,0:T(8,128)(2,1)S(1)}, bf16[1,4,1,128,128]{4,3,2,1,0:T(8,128)(2,1)}, u32[]{:S(2)}) copy-start(bf16[1,4,1,128,128]{4,3,2,1,0:T(8,128)(2,1)} %param.5) | copy-start | bytes 393220
  1.6 0.7 %copy-start.2 = (s32[1024]{0:T(1024)S(1)}, s32[1024]{0:T(1024)}, u32[]{:S(2)}) copy-start(s32[1024]{0:T(1024)} %param.9) | copy-start | bytes 12292

commit v2 on v1

--- a/solution.py
+++ b/solution.py
@@ -8,14 +8,17 @@
 from jax.sharding import PartitionSpec as P
 
 MESH = pl.DeviceIdType.MESH
-SLOTS = (0, 3, 1, 2)
+CHARGE = (0, 1, -1, 0)
+SITE2_PIECES = ((0, 0, 4), (1, 0, 1), (1, 2, 4), (2, 1, 3), (3, 0, 2), (3, 3, 4))
 
 
 def tree_kernel(
     seg_count, sec_count,
-    blocks_hbm, left_ref, right_ref, occ_ref, start_ref, out_ref,
-    mats, x_in, y_out, big_out, l_in, r_in, occ_in, one_l, one_r, sel_r, fin,
-    mat_sem, ch_send, ch_recv, l_recv, occ_send, occ_recv, fin_send, fin_recv,
+    blocks_hbm, left_hbm, right_hbm, occ_hbm, start_hbm, out_ref,
+    mats, gath, cross, x_in, z_in, y_out, left_out, left_in,
+    edge, occ_in, start_in, one_l, one_r, sel_r, fin,
+    load_sem, edge_sem, occ_sem, start_sem, ch_send, ch_recv, z_recv, gath_send, gath_recv,
+    l_send, l_recv, occ_send, occ_recv, fin_send, fin_recv,
 ):
     seg = lax.axis_index("seg")
     sec = lax.axis_index("sec")
@@ -26,40 +29,18 @@
     near = (sec, up, down)
     hub = half
 
-    load = pltpu.make_async_copy(blocks_hbm, mats, mat_sem)
-    load.start()
-
+    def turned(step):
+        return lax.rem(sec + step, sec_count)
+
+    load = pltpu.make_async_copy(blocks_hbm, mats, load_sem)
     barrier = pltpu.get_barrier_semaphore()
 
     def greet(seg_to, sec_to):
         pl.semaphore_signal(barrier, inc=1, device_id=(seg_to, sec_to), device_id_type=MESH)
 
-    @pl.when(seg == hub)
-    def _():
-        for i in range(seg_count):
-            if i != hub:
-                greet(i, sec)
-        for i in (hub - 1, hub + 1):
-            greet(i, up)
-            greet(i, down)
-        for step in range(1, sec_count):
-            greet(hub, lax.rem(sec + step, sec_count))
-
-    @pl.when(seg != hub)
-    def _():
-        @pl.when(jnp.logical_and(seg >= 1, seg < last))
-        def _():
-            before = jnp.where(seg < half, seg - 1, seg + 1)
-            for place in near:
-                greet(before, place)
-
-        @pl.when(seg == last)
-        def _():
-            greet(last, up)
-            greet(last, down)
-
-        for place in range(sec_count):
-            greet(hub, place)
+    def greet_hubs():
+        for step in range(sec_count):
+            greet(hub, turned(step))
 
     def send(src, dst, send_sem, recv_sem, seg_to, sec_to):
         copy = pltpu.make_async_remote_copy(
@@ -76,7 +57,7 @@
         ).wait_recv()
 
     def send_occ():
-        return send(occ_ref, occ_in.at[seg], occ_send, occ_recv.at[seg], hub, sec)
+        return send(occ_hbm, occ_in.at[seg], occ_send, occ_recv.at[seg], hub, sec)
 
     rows16 = lax.broadcasted_iota(jnp.int32, (16, 128), 0)
 
@@ -86,101 +67,148 @@
             total = jnp.where(index == n, parts[n], total)
         return total
 
-    def left_products(x):
-        return [
-            jnp.dot(x, mats[n], preferred_element_type=jnp.float32).astype(jnp.bfloat16)
-            for n in SLOTS
-        ]
-
-    def left_send(out, into, sems):
-        return (
-            send(out.at[0:2], into.at[0:2], ch_send.at[0], sems.at[0], seg + 1, sec),
-            send(out.at[2:3], into.at[2:3], ch_send.at[1], sems.at[1], seg + 1, up),
-            send(out.at[3:4], into.at[3:4], ch_send.at[2], sems.at[2], seg + 1, down),
-        )
-
-    def left_wait(into, sems):
-        arrived(into.at[0:2], sems.at[0])
-        arrived(into.at[2:3], sems.at[1])
-        arrived(into.at[3:4], sems.at[2])
-
-    def left_slots():
-        by_n = [None] * 4
-        for place, n in enumerate(SLOTS):
-            by_n[n] = x_in[place]
-        return by_n
-
-    def f32(parts):
-        return [part.astype(jnp.float32) for part in parts]
+    def left_mul(x, block):
+        return jnp.dot(x, block, preferred_element_type=jnp.float32)
+
+    def right_mul(x, block):
+        return lax.dot_general(
+            x, block, (((1,), (1,)), ((), ())), preferred_element_type=jnp.float32
+        )
+
+    def rounded(x):
+        return x.astype(jnp.bfloat16)
 
     def right_products(parts):
-        return [
-            lax.dot_general(
-                parts[place], mats[n], (((1,), (1,)), ((), ())),
-                preferred_element_type=jnp.float32,
+        return [right_mul(parts[place], mats[n]) for n, place in enumerate((0, 1, 2, 0))]
+
+    def to_all(out, seg_to):
+        copies = ()
+        for step in range(sec_count):
+            slot = (sec_count - step) % sec_count
+            copies += (
+                send(out, z_in.at[slot], ch_send.at[step], z_recv.at[slot], seg_to, turned(step)),
             )
-            for n, place in enumerate((0, 1, 2, 0))
-        ]
-
-    def right_send(out, into):
-        return (
-            send(out, into.at[0], ch_send.at[0], ch_recv.at[0], seg - 1, sec),
-            send(out, into.at[2], ch_send.at[1], ch_recv.at[2], seg - 1, up),
-            send(out, into.at[1], ch_send.at[2], ch_recv.at[1], seg - 1, down),
-        )
-
-    def right_wait(into):
-        for place in range(3):
-            arrived(into.at[place], ch_recv.at[place])
+        return copies
 
     def finish(copies):
         for copy in copies:
             copy.wait_send()
 
-    def edge_rows(ref):
-        return jnp.broadcast_to(ref[...].astype(jnp.float32), (16, 128)).astype(jnp.bfloat16)
+    def edge_load(ref):
+        copy = pltpu.make_async_copy(ref, edge, edge_sem)
+        copy.start()
+        return copy
+
+    def edge_rows():
+        return rounded(jnp.broadcast_to(edge[...].astype(jnp.float32), (16, 128)))
 
     @pl.when(seg == 0)
     def _():
+        edges = edge_load(left_hbm)
+        load.start()
+        greet_hubs()
+        edges.wait()
+        load.wait()
+        x = edge_rows()
+        for place, n in enumerate((0, 3, 1, 2)):
+            y_out[place] = rounded(left_mul(x, mats[n]))
         pl.semaphore_wait(barrier, 4)
+        copies = (
+            send(y_out.at[2:3], x_in.at[2:3], ch_send.at[1], ch_recv.at[1], 1, up),
+            send(y_out.at[3:4], x_in.at[3:4], ch_send.at[2], ch_recv.at[2], 1, down),
+            send(y_out.at[0:2], x_in.at[0:2], ch_send.at[0], ch_recv.at[0], 1, sec),
+        )
+        occ = send_occ()
+        finish(copies + (occ,))
+
+    @pl.when(seg == 1)
+    def _():
+        for place in near:
+            greet(0, place)
+        greet_hubs()
+        load.start()
+        pl.semaphore_wait(barrier, 5)
+        occ = send_occ()
         load.wait()
-        for place, part in enumerate(left_products(edge_rows(left_ref))):
-            y_out[place] = part
-        copies = left_send(y_out, x_in, ch_recv)
+        arrived(x_in.at[0:2], ch_recv.at[0])
+        arrived(x_in.at[2:3], ch_recv.at[1])
+        arrived(x_in.at[3:4], ch_recv.at[2])
+        parts = [x_in[place].astype(jnp.float32) for place in (0, 2, 3, 1)]
+        x = rounded(pick(lax.rem(rows16, 4), parts))
+        parts = [left_mul(x, mats[n]) for n in range(4)]
+        y_out[0] = rounded(pick(lax.div(rows16, 4), parts))
+        finish(to_all(y_out.at[0], 3) + (occ,))
+
+    @pl.when(seg == 2)
+    def _():
+        greet_hubs()
+        pl.semaphore_wait(barrier, 5)
+        copies = ()
+        for place, (turn, low, high) in enumerate(SITE2_PIECES):
+            copies += (
+                send(
+                    blocks_hbm.at[low:high], gath.at[turn, low:high], gath_send.at[place],
+                    gath_recv.at[place], 3, turned(sec_count - turn),
+                ),
+            )
         occ = send_occ()
         finish(copies + (occ,))
 
-    @pl.when(jnp.logical_or(seg == 1, seg == 2))
-    def _():
-        pl.semaphore_wait(barrier, 4)
+    @pl.when(seg == 3)
+    def _():
+        greet(3, up)
+        greet(3, down)
+        for step in range(sec_count):
+            greet(2, turned(step))
+        for step in range(sec_count):
+            greet(1, turned(step))
+        greet_hubs()
+        load.start()
+        pl.semaphore_wait(barrier, 3)
+        copies = (
+            send(blocks_hbm.at[1:2], cross.at[0:1], ch_send.at[0], ch_recv.at[0], 3, up),
+            send(blocks_hbm.at[2:3], cross.at[1:2], ch_send.at[1], ch_recv.at[1], 3, down),
+        )
         occ = send_occ()
         load.wait()
-        left_wait(x_in, ch_recv)
-        index = jnp.where(seg == 1, lax.rem(rows16, 4), lax.div(rows16, 4))
-        x = pick(index, f32(left_slots())).astype(jnp.bfloat16)
-        for place, part in enumerate(left_products(x)):
-            y_out[place] = part
-        copies = left_send(y_out, x_in, ch_recv)
-        finish(copies + (occ,))
-
-    @pl.when(seg == 3)
-    def _():
-        pl.semaphore_wait(barrier, 3)
-        occ = send_occ()
-        load.wait()
-        left_wait(x_in, ch_recv)
-        x = jnp.concatenate(left_slots(), axis=0)
-        for place, part in enumerate(left_products(x)):
-            big_out[place] = part
-        copies = left_send(big_out, l_in, l_recv)
-        finish(copies + (occ,))
+        arrived(cross.at[0:1], ch_recv.at[0])
+        arrived(cross.at[1:2], ch_recv.at[1])
+        for place, (turn, low, high) in enumerate(SITE2_PIECES):
+            arrived(gath.at[turn, low:high], gath_recv.at[place])
+        for slot in range(4):
+            arrived(z_in.at[slot], z_recv.at[slot])
+        heads = [z_in[slot].astype(jnp.float32) for slot in range(4)]
+        block_rows = lax.div(rows16, 4)
+        bond2 = [
+            rounded(pick(block_rows, [heads[(turn - CHARGE[n]) % 4] for n in range(4)]))
+            for turn in range(4)
+        ]
+        bond3 = {}
+        for turn in (0, -1, 1):
+            parts = []
+            for n in range(4):
+                source = (turn - CHARGE[n]) % 4
+                parts.append(rounded(left_mul(bond2[source], gath[source, n])))
+            bond3[turn] = jnp.concatenate(parts, axis=0)
+        blocks3 = (mats[0], cross[0], cross[1], mats[3])
+        for n in range(4):
+            part = left_mul(bond3[-CHARGE[n]], blocks3[n])
+            left_out[n * 64:(n + 1) * 64, :] = rounded(part)
+        final = send(left_out, left_in, l_send, l_recv, hub, sec)
+        finish(copies + (occ, final))
 
     @pl.when(seg == last)
     def _():
-        own = edge_rows(right_ref)
+        edges = edge_load(right_hbm)
+        greet(last, up)
+        greet(last, down)
+        greet_hubs()
+        load.start()
+        edges.wait()
+        own = edge_rows()
         y_out[0] = own
         pl.semaphore_wait(barrier, 6)
-        edges = (
+        copies = (
             send(y_out.at[0], x_in.at[2], ch_send.at[0], ch_recv.at[2], seg, up),
             send(y_out.at[0], x_in.at[1], ch_send.at[1], ch_recv.at[1], seg, down),
         )
@@ -189,52 +217,74 @@
         arrived(x_in.at[1], ch_recv.at[1])
         arrived(x_in.at[2], ch_recv.at[2])
         parts = right_products((own, x_in[1], x_in[2]))
-        y_out[1] = pick(lax.rem(rows16, 4), parts).astype(jnp.bfloat16)
-        finish(edges)
-        copies = right_send(y_out.at[1], x_in)
+        y_out[1] = rounded(pick(lax.rem(rows16, 4), parts))
+        finish(copies)
+        copies = (
+            send(y_out.at[1], x_in.at[2], ch_send.at[1], ch_recv.at[2], seg - 1, up),
+            send(y_out.at[1], x_in.at[1], ch_send.at[2], ch_recv.at[1], seg - 1, down),
+            send(y_out.at[1], x_in.at[0], ch_send.at[0], ch_recv.at[0], seg - 1, sec),
+        )
         finish(copies + (occ,))
 
     @pl.when(seg == 6)
     def _():
+        for place in near:
+            greet(last, place)
+        greet_hubs()
+        load.start()
         pl.semaphore_wait(barrier, 4)
         occ = send_occ()
         load.wait()
-        right_wait(x_in)
+        for place in range(3):
+            arrived(x_in.at[place], ch_recv.at[place])
         parts = right_products((x_in[0], x_in[1], x_in[2]))
-        y_out[0] = pick(lax.div(rows16, 4), parts).astype(jnp.bfloat16)
-        copies = right_send(y_out.at[0], x_in)
+        y_out[0] = rounded(pick(lax.div(rows16, 4), parts))
+        finish(to_all(y_out.at[0], hub) + (occ,))
+
+    @pl.when(seg == 5)
+    def _():
+        greet_hubs()
+        pl.semaphore_wait(barrier, 3)
+        copies = (
+            send(blocks_hbm, gath.at[2], gath_send.at[1], gath_recv.at[2], hub, up),
+            send(blocks_hbm, gath.at[1], gath_send.at[2], gath_recv.at[1], hub, down),
+            send(blocks_hbm, gath.at[0], gath_send.at[0], gath_recv.at[0], hub, sec),
+        )
+        occ = send_occ()
         finish(copies + (occ,))
 
-    @pl.when(seg == 5)
-    def _():
-        pl.semaphore_wait(barrier, 3)
-        occ = send_occ()
-        load.wait()
-        right_wait(x_in)
-        parts = right_products((x_in[0], x_in[1], x_in[2]))
-        for n in range(4):
-            big_out[0, n * 16:(n + 1) * 16, :] = parts[n].astype(jnp.bfloat16)
-        copies = right_send(big_out.at[0], r_in)
-        finish(copies + (occ,))
-
     @pl.when(seg == hub)
     def _():
+        for place in near:
+            greet(hub + 1, place)
+        for i in (0, 1, 2, 3, last):
+            greet(i, sec)
+        for step in range(sec_count):
+            greet(hub + 2, turned(step))
+        for step in range(1, sec_count):
+            greet(hub, turned(step))
+        load.start()
+        own_occ = pltpu.make_async_copy(occ_hbm, occ_in.at[hub], occ_sem)
+        own_occ.start()
+        start = pltpu.make_async_copy(start_hbm, start_in, start_sem)
+        start.start()
+        own_occ.wait()
+        start.wait()
         for i in range(seg_count):
             if i != hub:
                 arrived(occ_in.at[i], occ_recv.at[i])
-        occ = [occ_ref[...] if i == hub else occ_in[i] for i in range(seg_count)]
-        middle = start_ref[...]
+        occ = [occ_in[i] for i in range(seg_count)]
+        middle = start_in[...]
         for n in occ[:half]:
             middle = middle + jnp.where(n == 1, 1, 0) - jnp.where(n == 2, 1, 0)
-        slot = jnp.where(occ[3] == 0, 0, jnp.where(occ[3] == 3, 1, occ[3] + 1))
-        key_l = slot * 64 + occ[2] * 16 + occ[1] * 4 + occ[0]
+        key_l = occ[3] * 64 + occ[2] * 16 + occ[1] * 4 + occ[0]
         key_l = jnp.where(lax.rem(middle + 2 * sec_count, sec_count) == sec, key_l, -1)
         key_r = occ[4] * 64 + occ[5] * 16 + occ[6] * 4 + occ[7]
         rows = lax.broadcasted_iota(jnp.int32, (256, 128), 0)
         for j in range(8):
             here = slice(j * 128, (j + 1) * 128)
-            one_r[:, here] = jnp.where(rows == key_r[j:j + 1, :], 1.0, 0.0).astype(jnp.bfloat16)
-            one_l[:, here] = jnp.where(rows == key_l[j:j + 1, :], 1.0, 0.0).astype(jnp.bfloat16)
+            one_r[:, here] = rounded(jnp.where(rows == key_r[j:j + 1, :], 1.0, 0.0))
+            one_l[:, here] = rounded(jnp.where(rows == key_l[j:j + 1, :], 1.0, 0.0))
         load.wait()
 
         def select(vectors, one_hot):
@@ -243,27 +293,43 @@
                 preferred_element_type=jnp.float32,
             )
 
-        right_wait(r_in)
-        parts = right_products((r_in[0], r_in[1], r_in[2]))
-        right = jnp.concatenate([part.astype(jnp.bfloat16) for part in parts], axis=0)
+        for place in range(3):
+            arrived(gath.at[place], gath_recv.at[place])
+        for slot in range(4):
+            arrived(z_in.at[slot], z_recv.at[slot])
+        bond6 = [z_in[slot] for slot in range(4)]
+        bond5 = []
+        for place, turn in enumerate((0, 1, -1)):
+            parts = [
+                rounded(right_mul(bond6[(turn + CHARGE[n]) % 4], gath[place, n]))
+                for n in range(4)
+            ]
+            bond5.append(jnp.concatenate(parts, axis=0))
+        right = jnp.concatenate([rounded(part) for part in right_products(bond5)], axis=0)
         sel_r[...] = select(right, one_r)
-        left_wait(l_in, l_recv)
-        left = jnp.concatenate([l_in[place] for place in range(4)], axis=0)
-        value = jnp.sum(select(left, one_l) * sel_r[...], axis=0, keepdims=True)
+        arrived(left_in, l_recv)
+        value = jnp.sum(select(left_in[...], one_l) * sel_r[...], axis=0, keepdims=True)
         for j in range(8):
             fin[sec, j:j + 1, :] = value[:, j * 128:(j + 1) * 128]
         count = seg_count * sec_count
         pl.semaphore_wait(barrier, count - 1)
-        me = seg * sec_count + sec
-        copies = []
-        for step in range(1, count):
-            to = lax.rem(me + step, count)
-            copies.append(
+        copies = ()
+
+        def spread(seg_to, sec_to):
+            return (
                 send(
-                    fin.at[sec], fin.at[sec], fin_send.at[step - 1], fin_recv.at[sec],
-                    lax.div(to, sec_count), lax.rem(to, sec_count),
-                )
+                    fin.at[sec], fin.at[sec], fin_send.at[len(copies)], fin_recv.at[sec],
+                    seg_to, sec_to,
+                ),
             )
+
+        for j in range(sec_count):
+            place = jnp.where(sec < sec_count // 2, sec_count - 1 - j, j)
+            for i in range(seg_count):
+                if i != hub:
+                    copies += spread(i, place)
+            if j > 0:
+                copies += spread(hub, turned(j))
         finish(copies)
 
     for place in range(sec_count):
@@ -277,37 +343,43 @@
 def tree_device(blocks, left_edge, right_edge, occupation, start_sector):
     seg_count = lax.axis_size("seg")
     sec_count = lax.axis_size("sec")
-    vmem = pl.BlockSpec(memory_space=pltpu.VMEM)
+    hbm = pl.BlockSpec(memory_space=pl.ANY)
     dma = pltpu.SemaphoreType.DMA
     bf16, f32, i32 = jnp.bfloat16, jnp.float32, jnp.int32
     values = pl.pallas_call(
         functools.partial(tree_kernel, seg_count, sec_count),
         out_shape=jax.ShapeDtypeStruct((8, 128), f32),
-        in_specs=[pl.BlockSpec(memory_space=pl.ANY)] + [vmem] * 4,
-        out_specs=vmem,
+        in_specs=[hbm] * 5,
+        out_specs=pl.BlockSpec(memory_space=pltpu.VMEM),
         scratch_shapes=[
             pltpu.VMEM((4, 128, 128), bf16),
+            pltpu.VMEM((4, 4, 128, 128), bf16),
+            pltpu.VMEM((2, 128, 128), bf16),
             pltpu.VMEM((4, 16, 128), bf16),
             pltpu.VMEM((4, 16, 128), bf16),
-            pltpu.VMEM((4, 64, 128), bf16),
-            pltpu.VMEM((4, 64, 128), bf16),
-            pltpu.VMEM((3, 64, 128), bf16),
+            pltpu.VMEM((4, 16, 128), bf16),
+            pltpu.VMEM((256, 128), bf16),
+            pltpu.VMEM((256, 128), bf16),
+            pltpu.VMEM((1, 128), bf16),
             pltpu.VMEM((8, 8, 128), i32),
+            pltpu.VMEM((8, 128), i32),
             pltpu.VMEM((256, 1024), bf16),
             pltpu.VMEM((256, 1024), bf16),
             pltpu.VMEM((128, 1024), f32),
             pltpu.VMEM((4, 8, 128), f32),
-            dma,
+            dma, dma, dma, dma,
+            dma((4,)),
             dma((3,)),
-            dma((3,)),
-            dma((3,)),
-            dma,
+            dma((4,)),
+            dma((6,)),
+            dma((6,)),
+            dma, dma, dma,
             dma((8,)),
             dma((seg_count * sec_count - 1,)),
             dma((4,)),
         ],
         compiler_params=pltpu.CompilerParams(
-            collective_id=0, has_side_effects=True, vmem_limit_bytes=16 * 1024 * 1024
+            collective_id=0, has_side_effects=True, vmem_limit_bytes=60 * 1024 * 1024
         ),
     )(
         blocks.reshape(4, 128, 128),

time: 27.5 us -> 23.6 us (0.86)
  Pallas kernels: 24.4 us -> 22.2 us
  local copies, waits for them, and re-layouts: 2.88 us -> 1.28 us
    pallas_call x1, Pallas kernels: 24.4 us -> 22.2 us  [tree_device(): pl.pallas_call(functools.partial(tree_kernel, seg_count, sec_count), out_...]
    unnamed x11 -> x1, local copies, waits for them, and re-layouts: 2.88 us -> 1.28 us
where the time goes in v2:
time: 23.6 us; the launch traced here: 23.5 us
  Pallas kernels  22.2 us (94%)
  local copies, waits for them, and re-layouts  1.28 us (5%)
    pallas_call x1, Pallas kernels, tree_device(): pl.pallas_call(functools.partial(tree_kernel, seg_count, sec_count), out_...  22.2 us
    unnamed x1, local copies, waits for them, and re-layouts  1.28 us

profile of v2, /device:TPU:0, one launch (start us, length us, event | category | flops | bytes accessed | tf_op | source)
XLA Modules:
  0.0 23.5 jit_solution(9267896619148205179)
XLA Ops:
  0.0 22.2 %shard_map.55 = f32[8,128]{1,0:T(8,128)} custom-call(bf16[4,128,128]{2,1,0:T(8,128)(2,1)} %bitcast.4, bf16[1,128]{1,0:T(2,128)(2,1)} %left_hbm.1, bf16[1,128]{1,0:T(2,128)(2,1)} %right_hbm.1, s32[8,128]{1,0:T(8,128)} %bitcast.6, s32[8,128]{1,0:T(8,128)} %bitcast.7), custom_call_target="tpu_custom_call" | custom-call | tf_op jit(solution)/shard_map/pallas_call | solution.py:349
  22.2 1.3 %copy.7 = f32[1024]{0:T(1024)} copy(f32[1024]{0:T(1024)} %bitcast.5) | data formatting | bytes 8192

commit v3 on v2

--- a/solution.py
+++ b/solution.py
@@ -16,7 +16,7 @@
     seg_count, sec_count,
     blocks_hbm, left_hbm, right_hbm, occ_hbm, start_hbm, out_ref,
     mats, gath, cross, x_in, z_in, y_out, left_out, left_in,
-    edge, occ_in, start_in, one_l, one_r, sel_r, fin,
+    edge, ends, occ_in, start_in, one_l, one_r, sel_r, fin,
     load_sem, edge_sem, occ_sem, start_sem, ch_send, ch_recv, z_recv, gath_send, gath_recv,
     l_send, l_recv, occ_send, occ_recv, fin_send, fin_recv,
 ):
@@ -193,53 +193,74 @@
         blocks3 = (mats[0], cross[0], cross[1], mats[3])
         for n in range(4):
             part = left_mul(bond3[-CHARGE[n]], blocks3[n])
-            left_out[n * 64:(n + 1) * 64, :] = rounded(part)
-        final = send(left_out, left_in, l_send, l_recv, hub, sec)
-        finish(copies + (occ, final))
+            left_out[n] = rounded(part)
+            copies += (
+                send(left_out.at[n], left_in.at[n], l_send.at[n], l_recv.at[n], hub, sec),
+            )
+        finish(copies + (occ,))
 
     @pl.when(seg == last)
     def _():
         edges = edge_load(right_hbm)
-        greet(last, up)
-        greet(last, down)
+        for step in range(1, sec_count):
+            greet(last, turned(step))
+        greet(last - 1, sec)
         greet_hubs()
         load.start()
         edges.wait()
+        load.wait()
         own = edge_rows()
-        y_out[0] = own
-        pl.semaphore_wait(barrier, 6)
-        copies = (
-            send(y_out.at[0], x_in.at[2], ch_send.at[0], ch_recv.at[2], seg, up),
-            send(y_out.at[0], x_in.at[1], ch_send.at[1], ch_recv.at[1], seg, down),
-        )
-        occ = send_occ()
-        load.wait()
-        arrived(x_in.at[1], ch_recv.at[1])
-        arrived(x_in.at[2], ch_recv.at[2])
-        parts = right_products((own, x_in[1], x_in[2]))
-        y_out[1] = rounded(pick(lax.rem(rows16, 4), parts))
+        kept = jnp.where(
+            lax.rem(rows16, 4) == 0, right_mul(own, mats[0]), right_mul(own, mats[3])
+        )
+        ends[0, 0] = rounded(kept)
+        ends[0, 1] = own
+        pl.semaphore_wait(barrier, 7)
+        copies = ()
+        for step in (2, 1, 3):
+            copies += (
+                send(
+                    ends.at[0], ends.at[sec_count - step], ch_send.at[step],
+                    z_recv.at[sec_count - step], seg, turned(step),
+                ),
+            )
+        for place, to in ((1, up), (0, down)):
+            copies += (
+                send(
+                    blocks_hbm.at[1:3], gath.at[place, 1:3], gath_send.at[place],
+                    gath_recv.at[place], seg, to,
+                ),
+            )
+        occ = send_occ()
+        for slot in range(1, 4):
+            arrived(ends.at[slot], z_recv.at[slot])
+        arrived(gath.at[2], gath_recv.at[2])
+        for place in range(2):
+            arrived(gath.at[place, 1:3], gath_recv.at[place])
+        bond7 = []
+        for turn, ones, twos in (
+            (0, mats[1], mats[2]), (1, gath[0, 1], gath[0, 2]), (-1, gath[1, 1], gath[1, 2])
+        ):
+            kept = ends[turn % 4, 0].astype(jnp.float32)
+            parts = [
+                kept,
+                right_mul(ends[(turn + 1) % 4, 1], ones),
+                right_mul(ends[(turn - 1) % 4, 1], twos),
+                kept,
+            ]
+            bond7.append(rounded(pick(lax.rem(rows16, 4), parts)))
+        parts = [right_mul(bond7[place], gath[2, n]) for n, place in enumerate((0, 1, 2, 0))]
+        y_out[0] = rounded(pick(lax.div(rows16, 4), parts))
         finish(copies)
-        copies = (
-            send(y_out.at[1], x_in.at[2], ch_send.at[1], ch_recv.at[2], seg - 1, up),
-            send(y_out.at[1], x_in.at[1], ch_send.at[2], ch_recv.at[1], seg - 1, down),
-            send(y_out.at[1], x_in.at[0], ch_send.at[0], ch_recv.at[0], seg - 1, sec),
-        )
-        finish(copies + (occ,))
+        finish(to_all(y_out.at[0], hub) + (occ,))
 
     @pl.when(seg == 6)
     def _():
-        for place in near:
-            greet(last, place)
-        greet_hubs()
-        load.start()
-        pl.semaphore_wait(barrier, 4)
-        occ = send_occ()
-        load.wait()
-        for place in range(3):
-            arrived(x_in.at[place], ch_recv.at[place])
-        parts = right_products((x_in[0], x_in[1], x_in[2]))
-        y_out[0] = rounded(pick(lax.div(rows16, 4), parts))
-        finish(to_all(y_out.at[0], hub) + (occ,))
+        greet_hubs()
+        pl.semaphore_wait(barrier, 2)
+        copy = send(blocks_hbm, gath.at[2], gath_send.at[0], gath_recv.at[2], last, sec)
+        occ = send_occ()
+        finish((copy, occ))
 
     @pl.when(seg == 5)
     def _():
@@ -257,10 +278,10 @@
     def _():
         for place in near:
             greet(hub + 1, place)
-        for i in (0, 1, 2, 3, last):
+        for i in (0, 1, 2, 3, last - 1):
             greet(i, sec)
         for step in range(sec_count):
-            greet(hub + 2, turned(step))
+            greet(last, turned(step))
         for step in range(1, sec_count):
             greet(hub, turned(step))
         load.start()
@@ -307,8 +328,10 @@
             bond5.append(jnp.concatenate(parts, axis=0))
         right = jnp.concatenate([rounded(part) for part in right_products(bond5)], axis=0)
         sel_r[...] = select(right, one_r)
-        arrived(left_in, l_recv)
-        value = jnp.sum(select(left_in[...], one_l) * sel_r[...], axis=0, keepdims=True)
+        for n in range(4):
+            arrived(left_in.at[n], l_recv.at[n])
+        left = jnp.concatenate([left_in[n] for n in range(4)], axis=0)
+        value = jnp.sum(select(left, one_l) * sel_r[...], axis=0, keepdims=True)
         for j in range(8):
             fin[sec, j:j + 1, :] = value[:, j * 128:(j + 1) * 128]
         count = seg_count * sec_count
@@ -358,9 +381,10 @@
             pltpu.VMEM((4, 16, 128), bf16),
             pltpu.VMEM((4, 16, 128), bf16),
             pltpu.VMEM((4, 16, 128), bf16),
-            pltpu.VMEM((256, 128), bf16),
-            pltpu.VMEM((256, 128), bf16),
+            pltpu.VMEM((4, 64, 128), bf16),
+            pltpu.VMEM((4, 64, 128), bf16),
             pltpu.VMEM((1, 128), bf16),
+            pltpu.VMEM((4, 2, 16, 128), bf16),
             pltpu.VMEM((8, 8, 128), i32),
             pltpu.VMEM((8, 128), i32),
             pltpu.VMEM((256, 1024), bf16),
@@ -373,7 +397,9 @@
             dma((4,)),
             dma((6,)),
             dma((6,)),
-            dma, dma, dma,
+            dma((4,)),
+            dma((4,)),
+            dma,
             dma((8,)),
             dma((seg_count * sec_count - 1,)),
             dma((4,)),

time: 23.6 us -> 21.5 us (0.911)
  Pallas kernels: 22.2 us -> 20.1 us
    pallas_call x1, Pallas kernels: 22.2 us -> 20.1 us  [tree_device(): pl.pallas_call(functools.partial(tree_kernel, seg_count, sec_count), out_...]
where the time goes in v3:
time: 21.5 us; the launch traced here: 21.4 us
  Pallas kernels  20.1 us (93%)
  local copies, waits for them, and re-layouts  1.28 us (6%)
    pallas_call x1, Pallas kernels, tree_device(): pl.pallas_call(functools.partial(tree_kernel, seg_count, sec_count), out_...  20.1 us
    unnamed x1, local copies, waits for them, and re-layouts  1.28 us

profile of v3, /device:TPU:0, one launch (start us, length us, event | category | flops | bytes accessed | tf_op | source)
XLA Modules:
  0.0 21.4 jit_solution(5788168967893295997)
XLA Ops:
  0.0 20.1 %shard_map.55 = f32[8,128]{1,0:T(8,128)} custom-call(bf16[4,128,128]{2,1,0:T(8,128)(2,1)} %bitcast.4, bf16[1,128]{1,0:T(2,128)(2,1)} %left_hbm.1, bf16[1,128]{1,0:T(2,128)(2,1)} %right_hbm.1, s32[8,128]{1,0:T(8,128)} %bitcast.6, s32[8,128]{1,0:T(8,128)} %bitcast.7), custom_call_target="tpu_custom_call" | custom-call | tf_op jit(solution)/shard_map/pallas_call | solution.py:372
  20.1 1.3 %copy.7 = f32[1024]{0:T(1024)} copy(f32[1024]{0:T(1024)} %bitcast.5) | data formatting | bytes 8192

commit v4 on v3

--- a/solution.py
+++ b/solution.py
@@ -14,9 +14,9 @@
 
 def tree_kernel(
     seg_count, sec_count,
-    blocks_hbm, left_hbm, right_hbm, occ_hbm, start_hbm, out_ref,
+    blocks_hbm, left_hbm, right_hbm, occ_hbm, start_hbm, fin,
     mats, gath, cross, x_in, z_in, y_out, left_out, left_in,
-    edge, ends, occ_in, start_in, one_l, one_r, sel_r, fin,
+    edge, ends, occ_in, start_in, one_l, one_r, sel_r, part,
     load_sem, edge_sem, occ_sem, start_sem, ch_send, ch_recv, z_recv, gath_send, gath_recv,
     l_send, l_recv, occ_send, occ_recv, fin_send, fin_recv,
 ):
@@ -276,12 +276,13 @@
 
     @pl.when(seg == hub)
     def _():
-        for place in near:
+        for step in (2, 1, 3, 0):
+            greet(last, turned(step))
+        greet(0, sec)
+        for place in (up, down, sec):
             greet(hub + 1, place)
-        for i in (0, 1, 2, 3, last - 1):
+        for i in (1, 2, 3, last - 1):
             greet(i, sec)
-        for step in range(sec_count):
-            greet(last, turned(step))
         for step in range(1, sec_count):
             greet(hub, turned(step))
         load.start()
@@ -333,15 +334,16 @@
         left = jnp.concatenate([left_in[n] for n in range(4)], axis=0)
         value = jnp.sum(select(left, one_l) * sel_r[...], axis=0, keepdims=True)
         for j in range(8):
-            fin[sec, j:j + 1, :] = value[:, j * 128:(j + 1) * 128]
+            part[j:j + 1, :] = value[:, j * 128:(j + 1) * 128]
         count = seg_count * sec_count
         pl.semaphore_wait(barrier, count - 1)
         copies = ()
+        own = pltpu.make_async_copy(part, fin.at[sec], occ_sem)
 
         def spread(seg_to, sec_to):
             return (
                 send(
-                    fin.at[sec], fin.at[sec], fin_send.at[len(copies)], fin_recv.at[sec],
+                    part, fin.at[sec], fin_send.at[len(copies)], fin_recv.at[sec],
                     seg_to, sec_to,
                 ),
             )
@@ -353,14 +355,14 @@
                     copies += spread(i, place)
             if j > 0:
                 copies += spread(hub, turned(j))
+        own.start()
         finish(copies)
+        own.wait()
 
     for place in range(sec_count):
         @pl.when(jnp.logical_or(seg != hub, sec != place))
         def _():
             arrived(fin.at[place], fin_recv.at[place])
-
-    out_ref[...] = (fin[0] + fin[1]) + (fin[2] + fin[3])
 
 
 def tree_device(blocks, left_edge, right_edge, occupation, start_sector):
@@ -371,9 +373,9 @@
     bf16, f32, i32 = jnp.bfloat16, jnp.float32, jnp.int32
     values = pl.pallas_call(
         functools.partial(tree_kernel, seg_count, sec_count),
-        out_shape=jax.ShapeDtypeStruct((8, 128), f32),
+        out_shape=jax.ShapeDtypeStruct((sec_count, 8, 128), f32),
         in_specs=[hbm] * 5,
-        out_specs=pl.BlockSpec(memory_space=pltpu.VMEM),
+        out_specs=hbm,
         scratch_shapes=[
             pltpu.VMEM((4, 128, 128), bf16),
             pltpu.VMEM((4, 4, 128, 128), bf16),
@@ -390,7 +392,7 @@
             pltpu.VMEM((256, 1024), bf16),
             pltpu.VMEM((256, 1024), bf16),
             pltpu.VMEM((128, 1024), f32),
-            pltpu.VMEM((4, 8, 128), f32),
+            pltpu.VMEM((8, 128), f32),
             dma, dma, dma, dma,
             dma((4,)),
             dma((3,)),
@@ -414,7 +416,7 @@
         occupation.reshape(8, 128),
         start_sector.reshape(8, 128),
     )
-    return values.reshape(1024)
+    return ((values[0] + values[1]) + (values[2] + values[3])).reshape(1024)
 
 
 def fits_tree(mesh, blocks, occupation):

time: 21.5 us -> 21.1 us (0.981)
  other arithmetic: 0 us -> 1.29 us
  local copies, waits for them, and re-layouts: 1.28 us -> 0 us
  Pallas kernels: 20.1 us -> 19.6 us
    add x0 -> x1, other arithmetic: none -> 1.29 us  [tree_device(): return (values[0] + values[1] + (values[2] + values[3])).reshape(1024)]
    unnamed x1 -> x0, local copies, waits for them, and re-layouts: 1.28 us -> none
    pallas_call x1, Pallas kernels: 20.1 us -> 19.6 us  [tree_device(): pl.pallas_call(functools.partial(tree_kernel, seg_count, sec_count), out_...]
where the time goes in v4:
time: 21.1 us; the launch traced here: 20.9 us
  Pallas kernels  19.6 us (93%)
  other arithmetic  1.29 us (6%)
    pallas_call x1, Pallas kernels, tree_device(): pl.pallas_call(functools.partial(tree_kernel, seg_count, sec_count), out_...  19.6 us
    add x1, other arithmetic, tree_device(): return (values[0] + values[1] + (values[2] + values[3])).reshape(1024)  1.29 us

profile of v4, /device:TPU:0, one launch (start us, length us, event | category | flops | bytes accessed | tf_op | source)
XLA Modules:
  0.0 20.9 jit_solution(5562276042922981857)
XLA Ops:
  0.0 19.6 %shard_map.55 = f32[4,8,128]{2,1,0:T(8,128)} custom-call(bf16[4,128,128]{2,1,0:T(8,128)(2,1)} %bitcast.5, bf16[1,128]{1,0:T(2,128)(2,1)} %left_hbm.1, bf16[1,128]{1,0:T(2,128)(2,1)} %right_hbm.1, s32[8,128]{1,0:T(8,128)} %bitcast.6, s32[8,128]{1,0:T(8,128)} %bitcast.7), custom_call_target="tpu_custom_call" | custom-call | tf_op jit(solution)/shard_map/pallas_call | solution.py:374
  19.6 1.3 %add_bitcast_fusion = f32[1024]{0:T(1024)} fusion(f32[4,8,128]{2,1,0:T(8,128)} %shard_map.55), kind=kLoop, calls=%fused_computation | loop fusion | flops 3072 | bytes 20480 | tf_op jit(solution)/shard_map/add | solution.py:419

commit v5 on v4

--- a/solution.py
+++ b/solution.py
@@ -9,14 +9,14 @@
 
 MESH = pl.DeviceIdType.MESH
 CHARGE = (0, 1, -1, 0)
-SITE2_PIECES = ((0, 0, 4), (1, 0, 1), (1, 2, 4), (2, 1, 3), (3, 0, 2), (3, 3, 4))
+SITE2_PIECES = ((1, 0, 1), (1, 2, 4), (2, 1, 3), (3, 0, 2), (3, 3, 4))
 
 
 def tree_kernel(
     seg_count, sec_count,
     blocks_hbm, left_hbm, right_hbm, occ_hbm, start_hbm, fin,
     mats, gath, cross, x_in, z_in, y_out, left_out, left_in,
-    edge, ends, occ_in, start_in, one_l, one_r, sel_r, part,
+    edge, ends, theirs, occ_in, start_in, one_l, one_r, sel_r, part,
     load_sem, edge_sem, occ_sem, start_sem, ch_send, ch_recv, z_recv, gath_send, gath_recv,
     l_send, l_recv, occ_send, occ_recv, fin_send, fin_recv,
 ):
@@ -27,7 +27,7 @@
     half = seg_count // 2
     last = seg_count - 1
     near = (sec, up, down)
-    hub = half
+    hub = half + 1
 
     def turned(step):
         return lax.rem(sec + step, sec_count)
@@ -77,9 +77,6 @@
 
     def rounded(x):
         return x.astype(jnp.bfloat16)
-
-    def right_products(parts):
-        return [right_mul(parts[place], mats[n]) for n, place in enumerate((0, 1, 2, 0))]
 
     def to_all(out, seg_to):
         copies = ()
@@ -137,42 +134,45 @@
         x = rounded(pick(lax.rem(rows16, 4), parts))
         parts = [left_mul(x, mats[n]) for n in range(4)]
         y_out[0] = rounded(pick(lax.div(rows16, 4), parts))
-        finish(to_all(y_out.at[0], 3) + (occ,))
+        finish(to_all(y_out.at[0], 2) + (occ,))
+
+    @pl.when(seg == 3)
+    def _():
+        greet_hubs()
+        pl.semaphore_wait(barrier, 4)
+        copies = ()
+        for n, to in ((1, up), (2, down), (0, sec), (3, sec)):
+            copies += (
+                send(
+                    blocks_hbm.at[n:n + 1], cross.at[n:n + 1], l_send.at[n], l_recv.at[n], 2, to
+                ),
+            )
+        occ = send_occ()
+        finish(copies + (occ,))
 
     @pl.when(seg == 2)
     def _():
-        greet_hubs()
-        pl.semaphore_wait(barrier, 5)
+        for step in range(1, sec_count):
+            greet(2, turned(step))
+        for place in near:
+            greet(3, place)
+        for step in range(sec_count):
+            greet(1, turned(step))
+        greet_hubs()
+        load.start()
+        pl.semaphore_wait(barrier, 4)
         copies = ()
         for place, (turn, low, high) in enumerate(SITE2_PIECES):
             copies += (
                 send(
                     blocks_hbm.at[low:high], gath.at[turn, low:high], gath_send.at[place],
-                    gath_recv.at[place], 3, turned(sec_count - turn),
+                    gath_recv.at[place], 2, turned(sec_count - turn),
                 ),
             )
         occ = send_occ()
-        finish(copies + (occ,))
-
-    @pl.when(seg == 3)
-    def _():
-        greet(3, up)
-        greet(3, down)
-        for step in range(sec_count):
-            greet(2, turned(step))
-        for step in range(sec_count):
-            greet(1, turned(step))
-        greet_hubs()
-        load.start()
-        pl.semaphore_wait(barrier, 3)
-        copies = (
-            send(blocks_hbm.at[1:2], cross.at[0:1], ch_send.at[0], ch_recv.at[0], 3, up),
-            send(blocks_hbm.at[2:3], cross.at[1:2], ch_send.at[1], ch_recv.at[1], 3, down),
-        )
-        occ = send_occ()
         load.wait()
-        arrived(cross.at[0:1], ch_recv.at[0])
-        arrived(cross.at[1:2], ch_recv.at[1])
+        for n in range(4):
+            arrived(cross.at[n:n + 1], l_recv.at[n])
         for place, (turn, low, high) in enumerate(SITE2_PIECES):
             arrived(gath.at[turn, low:high], gath_recv.at[place])
         for slot in range(4):
@@ -188,11 +188,10 @@
             parts = []
             for n in range(4):
                 source = (turn - CHARGE[n]) % 4
-                parts.append(rounded(left_mul(bond2[source], gath[source, n])))
+                parts.append(rounded(left_mul(bond2[source], mats[n] if source == 0 else gath[source, n])))
             bond3[turn] = jnp.concatenate(parts, axis=0)
-        blocks3 = (mats[0], cross[0], cross[1], mats[3])
         for n in range(4):
-            part = left_mul(bond3[-CHARGE[n]], blocks3[n])
+            part = left_mul(bond3[-CHARGE[n]], cross[n])
             left_out[n] = rounded(part)
             copies += (
                 send(left_out.at[n], left_in.at[n], l_send.at[n], l_recv.at[n], hub, sec),
@@ -202,9 +201,6 @@
     @pl.when(seg == last)
     def _():
         edges = edge_load(right_hbm)
-        for step in range(1, sec_count):
-            greet(last, turned(step))
-        greet(last - 1, sec)
         greet_hubs()
         load.start()
         edges.wait()
@@ -215,81 +211,84 @@
         )
         ends[0, 0] = rounded(kept)
         ends[0, 1] = own
-        pl.semaphore_wait(barrier, 7)
+        pl.semaphore_wait(barrier, 5)
         copies = ()
-        for step in (2, 1, 3):
+        for step in (2, 1, 3, 0):
+            slot = (sec_count - step) % sec_count
             copies += (
                 send(
-                    ends.at[0], ends.at[sec_count - step], ch_send.at[step],
-                    z_recv.at[sec_count - step], seg, turned(step),
+                    ends.at[0], theirs.at[slot], ch_send.at[step], z_recv.at[slot],
+                    last - 1, turned(step),
                 ),
             )
-        for place, to in ((1, up), (0, down)):
+        for place, to in ((1, up), (0, down), (2, sec)):
             copies += (
                 send(
                     blocks_hbm.at[1:3], gath.at[place, 1:3], gath_send.at[place],
-                    gath_recv.at[place], seg, to,
+                    gath_recv.at[place], last - 1, to,
                 ),
             )
         occ = send_occ()
-        for slot in range(1, 4):
-            arrived(ends.at[slot], z_recv.at[slot])
-        arrived(gath.at[2], gath_recv.at[2])
-        for place in range(2):
+        finish(copies + (occ,))
+
+    @pl.when(seg == last - 1)
+    def _():
+        for step in (2, 1, 3, 0):
+            greet(last, turned(step))
+        greet_hubs()
+        load.start()
+        pl.semaphore_wait(barrier, 4)
+        occ = send_occ()
+        load.wait()
+        for slot in range(4):
+            arrived(theirs.at[slot], z_recv.at[slot])
+        for place in range(3):
             arrived(gath.at[place, 1:3], gath_recv.at[place])
         bond7 = []
         for turn, ones, twos in (
-            (0, mats[1], mats[2]), (1, gath[0, 1], gath[0, 2]), (-1, gath[1, 1], gath[1, 2])
+            (0, gath[2, 1], gath[2, 2]), (1, gath[0, 1], gath[0, 2]), (-1, gath[1, 1], gath[1, 2])
         ):
-            kept = ends[turn % 4, 0].astype(jnp.float32)
+            kept = theirs[turn % 4, 0].astype(jnp.float32)
             parts = [
                 kept,
-                right_mul(ends[(turn + 1) % 4, 1], ones),
-                right_mul(ends[(turn - 1) % 4, 1], twos),
+                right_mul(theirs[(turn + 1) % 4, 1], ones),
+                right_mul(theirs[(turn - 1) % 4, 1], twos),
                 kept,
             ]
             bond7.append(rounded(pick(lax.rem(rows16, 4), parts)))
-        parts = [right_mul(bond7[place], gath[2, n]) for n, place in enumerate((0, 1, 2, 0))]
+        parts = [right_mul(bond7[place], mats[n]) for n, place in enumerate((0, 1, 2, 0))]
         y_out[0] = rounded(pick(lax.div(rows16, 4), parts))
-        finish(copies)
         finish(to_all(y_out.at[0], hub) + (occ,))
 
-    @pl.when(seg == 6)
-    def _():
-        greet_hubs()
-        pl.semaphore_wait(barrier, 2)
-        copy = send(blocks_hbm, gath.at[2], gath_send.at[0], gath_recv.at[2], last, sec)
+    @pl.when(seg == half)
+    def _():
+        greet_hubs()
+        pl.semaphore_wait(barrier, 1)
+        copy = send(blocks_hbm, gath.at[0], gath_send.at[0], gath_recv.at[0], hub, sec)
         occ = send_occ()
         finish((copy, occ))
 
-    @pl.when(seg == 5)
-    def _():
-        greet_hubs()
-        pl.semaphore_wait(barrier, 3)
-        copies = (
-            send(blocks_hbm, gath.at[2], gath_send.at[1], gath_recv.at[2], hub, up),
-            send(blocks_hbm, gath.at[1], gath_send.at[2], gath_recv.at[1], hub, down),
-            send(blocks_hbm, gath.at[0], gath_send.at[0], gath_recv.at[0], hub, sec),
-        )
-        occ = send_occ()
-        finish(copies + (occ,))
-
     @pl.when(seg == hub)
     def _():
-        for step in (2, 1, 3, 0):
-            greet(last, turned(step))
-        greet(0, sec)
-        for place in (up, down, sec):
-            greet(hub + 1, place)
-        for i in (1, 2, 3, last - 1):
+        for i in (last, 0):
             greet(i, sec)
         for step in range(1, sec_count):
             greet(hub, turned(step))
+        for step in range(sec_count):
+            greet(last - 1, turned(step))
+        for i in (1, 2, 3, half):
+            greet(i, sec)
         load.start()
         own_occ = pltpu.make_async_copy(occ_hbm, occ_in.at[hub], occ_sem)
         own_occ.start()
         start = pltpu.make_async_copy(start_hbm, start_in, start_sem)
         start.start()
+        count = seg_count * sec_count
+        pl.semaphore_wait(barrier, count - 1)
+        given = (
+            send(blocks_hbm, gath.at[2], gath_send.at[1], gath_recv.at[2], hub, up),
+            send(blocks_hbm, gath.at[1], gath_send.at[2], gath_recv.at[1], hub, down),
+        )
         own_occ.wait()
         start.wait()
         for i in range(seg_count):
@@ -323,11 +322,12 @@
         bond5 = []
         for place, turn in enumerate((0, 1, -1)):
             parts = [
-                rounded(right_mul(bond6[(turn + CHARGE[n]) % 4], gath[place, n]))
+                rounded(right_mul(bond6[(turn + CHARGE[n]) % 4], gath[place, n] if place else mats[n]))
                 for n in range(4)
             ]
             bond5.append(jnp.concatenate(parts, axis=0))
-        right = jnp.concatenate([rounded(part) for part in right_products(bond5)], axis=0)
+        site4 = [right_mul(bond5[place], gath[0, n]) for n, place in enumerate((0, 1, 2, 0))]
+        right = jnp.concatenate([rounded(part) for part in site4], axis=0)
         sel_r[...] = select(right, one_r)
         for n in range(4):
             arrived(left_in.at[n], l_recv.at[n])
@@ -335,8 +335,6 @@
         value = jnp.sum(select(left, one_l) * sel_r[...], axis=0, keepdims=True)
         for j in range(8):
             part[j:j + 1, :] = value[:, j * 128:(j + 1) * 128]
-        count = seg_count * sec_count
-        pl.semaphore_wait(barrier, count - 1)
         copies = ()
         own = pltpu.make_async_copy(part, fin.at[sec], occ_sem)
 
@@ -356,7 +354,7 @@
             if j > 0:
                 copies += spread(hub, turned(j))
         own.start()
-        finish(copies)
+        finish(copies + given)
         own.wait()
 
     for place in range(sec_count):
@@ -379,13 +377,14 @@
         scratch_shapes=[
             pltpu.VMEM((4, 128, 128), bf16),
             pltpu.VMEM((4, 4, 128, 128), bf16),
-            pltpu.VMEM((2, 128, 128), bf16),
+            pltpu.VMEM((4, 128, 128), bf16),
             pltpu.VMEM((4, 16, 128), bf16),
             pltpu.VMEM((4, 16, 128), bf16),
             pltpu.VMEM((4, 16, 128), bf16),
             pltpu.VMEM((4, 64, 128), bf16),
             pltpu.VMEM((4, 64, 128), bf16),
             pltpu.VMEM((1, 128), bf16),
+            pltpu.VMEM((1, 2, 16, 128), bf16),
             pltpu.VMEM((4, 2, 16, 128), bf16),
             pltpu.VMEM((8, 8, 128), i32),
             pltpu.VMEM((8, 128), i32),

time: 21.1 us -> 21.3 us (level)
  no operation moved by 1% of the time
where the time goes in v5:
time: 21.3 us; the launch traced here: 21.1 us
  Pallas kernels  19.8 us (93%)
  other arithmetic  1.29 us (6%)
    pallas_call x1, Pallas kernels, tree_device(): pl.pallas_call(functools.partial(tree_kernel, seg_count, sec_count), out_...  19.8 us
    add x1, other arithmetic, tree_device(): return (values[0] + values[1] + (values[2] + values[3])).reshape(1024)  1.29 us

profile of v5, /device:TPU:0, one launch (start us, length us, event | category | flops | bytes accessed | tf_op | source)
XLA Modules:
  0.0 21.1 jit_solution(16776783118387281375)
XLA Ops:
  0.0 19.8 %shard_map.55 = f32[4,8,128]{2,1,0:T(8,128)} custom-call(bf16[4,128,128]{2,1,0:T(8,128)(2,1)} %bitcast.5, bf16[1,128]{1,0:T(2,128)(2,1)} %left_hbm.1, bf16[1,128]{1,0:T(2,128)(2,1)} %right_hbm.1, s32[8,128]{1,0:T(8,128)} %bitcast.6, s32[8,128]{1,0:T(8,128)} %bitcast.7), custom_call_target="tpu_custom_call" | custom-call | tf_op jit(solution)/shard_map/pallas_call | solution.py:372
  19.8 1.3 %add_bitcast_fusion = f32[1024]{0:T(1024)} fusion(f32[4,8,128]{2,1,0:T(8,128)} %shard_map.55), kind=kLoop, calls=%fused_computation | loop fusion | flops 3072 | bytes 20480 | tf_op jit(solution)/shard_map/add | solution.py:418

commit v6 on v4

--- a/solution.py
+++ b/solution.py
@@ -9,7 +9,7 @@
 
 MESH = pl.DeviceIdType.MESH
 CHARGE = (0, 1, -1, 0)
-SITE2_PIECES = ((0, 0, 4), (1, 0, 1), (1, 2, 4), (2, 1, 3), (3, 0, 2), (3, 3, 4))
+SITE2_PIECES = ((2, 1, 3), (1, 0, 1), (1, 2, 4), (3, 0, 2), (3, 3, 4), (0, 0, 4))
 
 
 def tree_kernel(
@@ -83,7 +83,7 @@
 
     def to_all(out, seg_to):
         copies = ()
-        for step in range(sec_count):
+        for step in (1, 3, 2, 0):
             slot = (sec_count - step) % sec_count
             copies += (
                 send(out, z_in.at[slot], ch_send.at[step], z_recv.at[slot], seg_to, turned(step)),

time: 21.1 us -> 21 us (level)
  no operation moved by 1% of the time
where the time goes in v6:
time: 21 us; the launch traced here: 20.8 us
  Pallas kernels  19.5 us (93%)
  other arithmetic  1.29 us (6%)
    pallas_call x1, Pallas kernels, tree_device(): pl.pallas_call(functools.partial(tree_kernel, seg_count, sec_count), out_...  19.5 us
    add x1, other arithmetic, tree_device(): return (values[0] + values[1] + (values[2] + values[3])).reshape(1024)  1.29 us

profile of v6, /device:TPU:0, one launch (start us, length us, event | category | flops | bytes accessed | tf_op | source)
XLA Modules:
  0.0 20.8 jit_solution(13652058035676691534)
XLA Ops:
  0.0 19.5 %shard_map.55 = f32[4,8,128]{2,1,0:T(8,128)} custom-call(bf16[4,128,128]{2,1,0:T(8,128)(2,1)} %bitcast.5, bf16[1,128]{1,0:T(2,128)(2,1)} %left_hbm.1, bf16[1,128]{1,0:T(2,128)(2,1)} %right_hbm.1, s32[8,128]{1,0:T(8,128)} %bitcast.6, s32[8,128]{1,0:T(8,128)} %bitcast.7), custom_call_target="tpu_custom_call" | custom-call | tf_op jit(solution)/shard_map/pallas_call | solution.py:374
  19.6 1.3 %add_bitcast_fusion = f32[1024]{0:T(1024)} fusion(f32[4,8,128]{2,1,0:T(8,128)} %shard_map.55), kind=kLoop, calls=%fused_computation | loop fusion | flops 3072 | bytes 20480 | tf_op jit(solution)/shard_map/add | solution.py:419
